TPU v7x, 32 devices: a whole 2x2x4 slice. The times are simulated.
32 devices in a mesh: gx: 8 (over y, x, core), gy: 4 (over z).
Axes of the slice: x: 2, y: 2, z: 4, core: 2. Of those that a mesh axis runs over, the one named last changes fastest.
Arguments:
- velocity: float32 [3, 128, 64, 512], P(None, 'gx', 'gy'), may hold values from -6 to 6
- stress: float32 [6, 128, 64, 512], P(None, 'gx', 'gy'), may hold values from -6 to 6
- pier_velocity: float32 [128, 16], P('gx', 'gy'), may hold values from -6 to 6
- buoyancy: float32 [128, 64, 512], P('gx', 'gy'), may hold values from 0.5 to 2
- layer: int32 [128], P('gx'), may hold values from 0 to 7, as said below
- lame_table: float32 [8], replicated, may hold values from 0.3 to 1.2
- shear_table: float32 [8], replicated, may hold values from 0.2 to 0.8
- relax_table: float32 [8], replicated, may hold values from 0.6 to 0.95
- impedance: float32 [16], P('gy'), may hold values from 0.5 to 2
- footprint: int32 [16, 16], replicated, may hold values from 0 to 32767, as said below
- damp_inverse: float32 [128, 128], replicated
Outputs:
- velocity_out: float32 [3, 128, 64, 512], P(None, 'gx', 'gy')
- stress_out: float32 [6, 128, 64, 512], P(None, 'gx', 'gy')
- pier_out: float32 [128, 16], P('gx', 'gy')
Inputs may be any that keep to these rules, and one draw needn't show every extreme that they name: `footprint`: row p lists the 16 cells of a square of 4 by 4 cells, row by row; squares may intersect and lie anywhere in the plane. `layer`: non-decreasing along depth; the first cell is in layer 0 and the last in layer 7.
All inputs are finite; a program needn't handle non-finite values.
Results may differ from a plain program's by a relative error of at most 0.00011.
Values sent between devices are 32-bit elements; how exact they have to be, the bound alone decides.
A program may use at most 192 MiB of HBM per device.

v0:
```python
import functools
import jax
import jax.numpy as jnp
from jax import lax
from jax.experimental import pallas as pl
from jax.experimental.pallas import tpu as pltpu
from jax.sharding import PartitionSpec as P

STEPS = 2
FOOT = 16


grid_ratio = 0.25
soil_gain = 0.2
pier_gain = 0.5


def extended(cells, sides, width):
    for axis, dim in sides:
        count = lax.axis_size(axis)
        ends = count - 1
        head = lax.slice_in_dim(cells, 0, width, axis=dim)
        tail = lax.slice_in_dim(cells, cells.shape[dim] - width, cells.shape[dim], axis=dim)
        cells = jnp.concatenate(
            [
                lax.ppermute(tail, axis, [(i, (i + 1) % count) for i in range(ends)]),
                cells,
                lax.ppermute(head, axis, [((i + 1) % count, i) for i in range(ends)]),
            ],
            axis=dim,
        )
    return cells


def forward_diff(padded, along):
    center = padded[1:-1, 1:-1, 1:-1]
    if along == 0:
        return padded[2:, 1:-1, 1:-1] - center
    if along == 1:
        return padded[1:-1, 2:, 1:-1] - center
    return padded[1:-1, 1:-1, 2:] - center


def backward_diff(padded, along):
    center = padded[1:-1, 1:-1, 1:-1]
    if along == 0:
        return center - padded[:-2, 1:-1, 1:-1]
    if along == 1:
        return center - padded[1:-1, :-2, 1:-1]
    return center - padded[1:-1, 1:-1, :-2]


def move_velocity(velocity, padded, buoyancy):
    scaled = grid_ratio * buoyancy
    first = velocity[0] + scaled * (
        backward_diff(padded[0], 2) + forward_diff(padded[3], 1) + forward_diff(padded[4], 0)
    )
    second = velocity[1] + scaled * (
        forward_diff(padded[3], 2) + backward_diff(padded[1], 1) + forward_diff(padded[5], 0)
    )
    third = velocity[2] + scaled * (
        forward_diff(padded[4], 2) + forward_diff(padded[5], 1) + backward_diff(padded[2], 0)
    )
    return jnp.stack([first, second, third])


def move_stress(stress, padded, lame_first, shear_mod, relax):
    strain_x = forward_diff(padded[0], 2)
    strain_y = forward_diff(padded[1], 1)
    strain_z = forward_diff(padded[2], 0)
    modulus = lame_first + 2.0 * shear_mod
    normal_x = relax * stress[0] + grid_ratio * (
        modulus * strain_x + lame_first * (strain_y + strain_z)
    )
    normal_y = relax * stress[1] + grid_ratio * (
        modulus * strain_y + lame_first * (strain_x + strain_z)
    )
    normal_z = relax * stress[2] + grid_ratio * (
        modulus * strain_z + lame_first * (strain_x + strain_y)
    )
    shear_xy = relax * stress[3] + grid_ratio * shear_mod * (
        backward_diff(padded[0], 1) + backward_diff(padded[1], 2)
    )
    shear_xz = relax * stress[4] + grid_ratio * shear_mod * (
        backward_diff(padded[0], 0) + backward_diff(padded[2], 2)
    )
    shear_yz = relax * stress[5] + grid_ratio * shear_mod * (
        backward_diff(padded[1], 0) + backward_diff(padded[2], 1)
    )
    return jnp.stack([normal_x, normal_y, normal_z, shear_xy, shear_xz, shear_yz])


def layer_values(layer, table):
    levels = jnp.arange(table.shape[0], dtype=jnp.int32)
    onehot = (layer[:, None] == levels[None, :]).astype(table.dtype)
    return jnp.sum(onehot * table[None, :], axis=1)[:, None, None]


def with_faces(fields):
    padded = extended(fields, (("gx", 1), ("gy", 2)), 1)
    return jnp.pad(padded, ((0, 0), (0, 0), (0, 0), (1, 1)))


def footprint_matches(cell_ids, footprint):
    piers = footprint.shape[0]
    equal = (cell_ids[:, None] == footprint.reshape(-1)[None, :]).astype(jnp.float32)
    return jnp.sum(equal.reshape(cell_ids.shape[0], piers, FOOT), axis=2)


def damp_columns(velocity, inverse):
    pencils = lax.all_to_all(velocity, "gx", split_axis=3, concat_axis=1, tiled=True)
    shape = pencils.shape
    flat = pencils.reshape(shape[0], shape[1], shape[2] * shape[3])
    damped = jnp.einsum("zk,fkm->fzm", inverse, flat, precision=lax.Precision.HIGHEST).reshape(
        shape
    )
    return lax.all_to_all(damped, "gx", split_axis=1, concat_axis=3, tiled=True)


def body(
    velocity,
    stress,
    pier_velocity,
    buoyancy,
    layer,
    lame_table,
    shear_table,
    relax_table,
    impedance,
    footprint,
    damp_inverse,
):
    depth_cells, side_cells, line_cells = (velocity.shape[1], velocity.shape[2], velocity.shape[3])
    own_piers = pier_velocity.shape[1]
    lame_first = layer_values(layer, lame_table)
    shear_mod = layer_values(layer, shear_table)
    relax = layer_values(layer, relax_table)
    row_start = lax.axis_index("gy") * side_cells
    cell_ids = row_start * line_cells + jnp.arange(side_cells * line_cells, dtype=jnp.int32)
    selector = footprint_matches(cell_ids, footprint)
    own_foot = lax.dynamic_slice_in_dim(footprint, lax.axis_index("gy") * own_piers, own_piers, 0)
    for time_step in range(STEPS):
        padded = with_faces(stress)
        velocity = move_velocity(velocity, padded, buoyancy)
        vertical = velocity[2].reshape(depth_cells, side_cells * line_cells)
        piece = lax.all_gather(velocity[2], "gy", axis=1, tiled=True)
        count = piece.shape[1]
        piece_ids = jnp.arange(count * line_cells, dtype=jnp.int32)
        picks = footprint_matches(piece_ids, own_foot)
        flat = piece.reshape(depth_cells, count * line_cells)
        summed = jnp.dot(
            flat, picks, precision=lax.Precision.HIGHEST, preferred_element_type=jnp.float32
        )
        mean_speed = summed / FOOT
        force = impedance[None, :] * (pier_velocity - mean_speed)
        pier_velocity = pier_velocity - pier_gain * force
        all_force = lax.all_gather(force, "gy", axis=1, tiled=True)
        pushed = jnp.dot(
            all_force,
            selector.T,
            precision=lax.Precision.HIGHEST,
            preferred_element_type=jnp.float32,
        )
        vertical = vertical + soil_gain * pushed
        velocity = jnp.stack(
            [velocity[0], velocity[1], vertical.reshape(depth_cells, side_cells, line_cells)]
        )
        velocity = damp_columns(velocity, damp_inverse)
        padded = with_faces(velocity)
        stress = move_stress(stress, padded, lame_first, shear_mod, relax)
    return (velocity, stress, pier_velocity)


SIDE = 4
LANES = 128
ROWS = 8
MESH = pl.DeviceIdType.MESH
Z_GHOSTS = ((2, -1), (4, 1), (5, 1))
Y_GHOSTS = ((1, -1), (3, 1), (5, 1))


def shift_x(a, ahead):
    lane = lax.broadcasted_iota(jnp.int32, a.shape, 1)
    width = a.shape[1]
    if ahead:
        return jnp.where(lane == width - 1, 0.0, pltpu.roll(a, width - 1, 1))
    return jnp.where(lane == 0, 0.0, pltpu.roll(a, 1, 1))


def fused(
    n, ng, v_hbm, s_hbm, b_hbm, layer_ref, lame_ref, shear_ref, relax_ref, foot_ref, w_ref, imp_ref, damp_ref,
    v_out, s_out, w_out,
    v_ext, s_ext, buoy, coef, acc, pin, pout, um, wbuf, sg_send, sg_recv, yg_send, yg_recv,
    load_sem, zs_send, zs_recv, cf_send, cf_recv, ys_send, ys_recv,
    f_send, f_recv, r_send, r_recv, u_send, u_recv, y_send, y_recv, o_sem,
):
    me = lax.axis_index("gx")
    g = lax.axis_index("gy")
    depth, side, line = buoy.shape
    tiles = line // LANES
    inner = pl.ds(ROWS, side)

    def piece(j):
        return (
            pl.ds(pl.multiple_of((j // tiles) * ROWS, ROWS), ROWS),
            pl.ds(pl.multiple_of((j % tiles) * LANES, LANES), LANES),
        )

    loads = {}
    for slot, f in enumerate((1, 3, 5, 2, 4, 0)):
        loads[("s", f)] = pltpu.make_async_copy(
            s_hbm.at[f], s_ext.at[f, pl.ds(1, depth), inner, :], load_sem.at[slot]
        )
    loads["b"] = pltpu.make_async_copy(b_hbm, buoy, load_sem.at[6])
    for f in range(3):
        loads[("v", f)] = pltpu.make_async_copy(
            v_hbm.at[f], v_ext.at[f, pl.ds(1, depth), inner, :], load_sem.at[7 + f]
        )
    for copy in loads.values():
        copy.start()

    plane = jnp.zeros((side, line), jnp.float32)
    for f, way in Z_GHOSTS:
        s_ext[f, 0 if way < 0 else depth + 1, inner, :] = plane
    edge = jnp.zeros((ROWS, line), jnp.float32)

    def clear(k, carry):
        for f, way in Y_GHOSTS:
            s_ext[f, k, pl.ds(0 if way < 0 else ROWS + side, ROWS), :] = edge
        for f in range(3 * STEPS):
            v_ext[f, k, pl.ds(0, ROWS), :] = edge
            v_ext[f, k, pl.ds(ROWS + side, ROWS), :] = edge
        return carry

    lax.fori_loop(0, depth + 2, clear, 0)
    for k in range(depth):
        for c, table in enumerate((lame_ref, shear_ref, relax_ref)):
            coef[c, k + 1] = jnp.full((ROWS, LANES), table[layer_ref[k]], jnp.float32)
    for c in range(3):
        coef[c, 0] = jnp.zeros((ROWS, LANES), jnp.float32)
        coef[c, depth + 1] = jnp.zeros((ROWS, LANES), jnp.float32)
        pout[c, 0] = jnp.zeros((ROWS, LANES), jnp.float32)
        pout[c, n * depth + 1] = jnp.zeros((ROWS, LANES), jnp.float32)

    barrier = pltpu.get_barrier_semaphore()
    for d in range(1, n):
        pl.semaphore_signal(
            barrier, inc=1, device_id=(lax.rem(me + d, n), g), device_id_type=MESH
        )
    for d in range(1, ng):
        pl.semaphore_signal(
            barrier, inc=1, device_id=(me, lax.rem(g + d, ng)), device_id_type=MESH
        )
    pl.semaphore_wait(barrier, n - 1 + ng - 1)

    def z_copy(i):
        f, way = Z_GHOSTS[i]
        return pltpu.make_async_remote_copy(
            src_ref=s_hbm.at[f, depth - 1 if way < 0 else 0],
            dst_ref=s_ext.at[f, 0 if way < 0 else depth + 1, inner, :],
            send_sem=zs_send.at[i],
            recv_sem=zs_recv.at[i],
            device_id=(me - way, g),
            device_id_type=MESH,
        )

    def c_copy(way):
        i = (way + 1) // 2
        return pltpu.make_async_remote_copy(
            src_ref=coef.at[:, depth if way < 0 else 1],
            dst_ref=coef.at[:, 0 if way < 0 else depth + 1],
            send_sem=cf_send.at[i],
            recv_sem=cf_recv.at[i],
            device_id=(me - way, g),
            device_id_type=MESH,
        )

    def y_stress(i):
        f, way = Y_GHOSTS[i]
        return pltpu.make_async_remote_copy(
            src_ref=sg_send.at[i],
            dst_ref=sg_recv.at[i],
            send_sem=ys_send.at[i],
            recv_sem=ys_recv.at[i],
            device_id=(me, g - way),
            device_id_type=MESH,
        )

    not_ends = {
        -1: (me > 0, me < n - 1, g > 0, g < ng - 1),
        1: (me < n - 1, me > 0, g < ng - 1, g > 0),
    }

    for i, (f, way) in enumerate(Z_GHOSTS):
        @pl.when(not_ends[way][1])
        def _(i=i):
            z_copy(i).start()
    for way in (-1, 1):
        @pl.when(not_ends[way][1])
        def _(way=way):
            c_copy(way).start()
    for i, (f, way) in enumerate(Y_GHOSTS):
        loads[("s", f)].wait()
        sg_send[i] = s_ext[f, pl.ds(1, depth), ROWS + side - 1 if way < 0 else ROWS, :]

        @pl.when(not_ends[way][3])
        def _(i=i):
            y_stress(i).start()
    for key, copy in loads.items():
        if key not in (("s", 1), ("s", 3), ("s", 5)):
            copy.wait()

    ids = lax.broadcasted_iota(jnp.int32, (side, LANES), 0) + g * side
    by_lane = lax.broadcasted_iota(jnp.int32, (side, LANES), 1)
    by_row = lax.broadcasted_iota(jnp.int32, (LANES, LANES), 0)
    first = jnp.full((side, LANES), -64, jnp.int32)
    begin = jnp.full((LANES, LANES), -64, jnp.int32)
    for p in range(foot_ref.shape[0]):
        first = jnp.where(by_lane == p, foot_ref[p, 0] // line, first)
        begin = jnp.where(by_row == p, foot_ref[p, 0] % line, begin)
    in_rows = jnp.where((ids >= first) & (ids < first + SIDE), 1.0, 0.0)
    across = lax.broadcasted_iota(jnp.int32, (LANES, line), 1)
    start = jnp.concatenate([begin] * tiles, axis=1)
    in_cols = jnp.where((across >= start) & (across < start + SIDE), 1.0, 0.0)

    for i, (f, way) in enumerate(Z_GHOSTS):
        @pl.when(not_ends[way][0])
        def _(i=i):
            z_copy(i).wait_recv()

        @pl.when(not_ends[way][1])
        def _(i=i):
            z_copy(i).wait_send()
    for way in (-1, 1):
        @pl.when(not_ends[way][0])
        def _(way=way):
            c_copy(way).wait_recv()

        @pl.when(not_ends[way][1])
        def _(way=way):
            c_copy(way).wait_send()
    for i, (f, way) in enumerate(Y_GHOSTS):
        @pl.when(not_ends[way][2])
        def _(i=i, f=f, way=way):
            y_stress(i).wait_recv()
            s_ext[f, pl.ds(1, depth), ROWS - 1 if way < 0 else ROWS + side, :] = sg_recv[i]

        @pl.when(not_ends[way][3])
        def _(i=i):
            y_stress(i).wait_send()

    def cells(ref, f, k, shift=0, begin=ROWS, rows=None):
        return ref[f, k, pl.ds(begin + shift, side if rows is None else rows), :]

    base = [0]

    def speed_x(i, carry):
        k = i + 1
        xx, xy, xz = cells(s_ext, 0, k), cells(s_ext, 3, k), cells(s_ext, 4, k)
        total = (xx - shift_x(xx, False)) + (cells(s_ext, 3, k, 1) - xy)
        total = total + (cells(s_ext, 4, k + 1) - xz)
        acc[0, i] = cells(v_ext, base[0] + 0, k) + (grid_ratio * buoy[i]) * total
        return carry

    def speed_y(i, carry):
        k = i + 1
        xy, yy, yz = cells(s_ext, 3, k), cells(s_ext, 1, k), cells(s_ext, 5, k)
        total = (shift_x(xy, True) - xy) + (yy - cells(s_ext, 1, k, -1))
        total = total + (cells(s_ext, 5, k + 1) - yz)
        acc[1, i] = cells(v_ext, base[0] + 1, k) + (grid_ratio * buoy[i]) * total
        return carry

    def speed_z(i, carry):
        k = i + 1
        xz, yz, zz = cells(s_ext, 4, k), cells(s_ext, 5, k), cells(s_ext, 2, k)
        total = (shift_x(xz, True) - xz) + (cells(s_ext, 5, k, 1) - yz)
        total = total + (zz - cells(s_ext, 2, k - 1))
        acc[2, i] = cells(v_ext, base[0] + 2, k) + (grid_ratio * buoy[i]) * total
        return carry

    def wide(c, k, rows):
        tile = jnp.concatenate([coef[c, k]] * tiles, axis=1)
        return jnp.concatenate([tile] * (rows // ROWS), axis=0)

    def normals(k, begin, rows, which=(0, 1, 2)):
        at = functools.partial(cells, begin=begin, rows=rows)
        lame, shear, relax = (wide(c, k, rows) for c in range(3))
        vx, vy, vz = at(v_ext, base[0] + 0, k), at(v_ext, base[0] + 1, k), at(v_ext, base[0] + 2, k)
        ex = shift_x(vx, True) - vx
        ey = at(v_ext, base[0] + 1, k, 1) - vy
        ez = at(v_ext, base[0] + 2, k + 1) - vz
        modulus = lame + 2.0 * shear
        for f in which:
            own, others = ((ex, ey + ez), (ey, ex + ez), (ez, ex + ey))[f]
            s_ext[f, k, pl.ds(begin, rows), :] = relax * at(s_ext, f, k) + grid_ratio * (
                modulus * own + lame * others
            )

    def shears(k, begin, rows, which):
        at = functools.partial(cells, begin=begin, rows=rows)
        shear, relax = grid_ratio * wide(1, k, rows), wide(2, k, rows)
        for f in which:
            if f == 3:
                vy = at(v_ext, base[0] + 1, k)
                strain = (at(v_ext, base[0] + 0, k) - at(v_ext, base[0] + 0, k, -1)) + (vy - shift_x(vy, False))
            elif f == 4:
                vz = at(v_ext, base[0] + 2, k)
                strain = (at(v_ext, base[0] + 0, k) - at(v_ext, base[0] + 0, k - 1)) + (vz - shift_x(vz, False))
            else:
                strain = (at(v_ext, base[0] + 1, k) - at(v_ext, base[0] + 1, k - 1)) + (
                    at(v_ext, base[0] + 2, k) - at(v_ext, base[0] + 2, k, -1)
                )
            s_ext[f, k, pl.ds(begin, rows), :] = relax * at(s_ext, f, k) + shear * strain

    def there(step, f, d):
        t = lax.rem(me + d, n)
        ys, xs = piece(t)
        src = acc.at[f, :, ys, xs]
        dst = pin.at[f, pl.ds(me * depth, depth)]
        if d == 0:
            return pltpu.make_async_copy(src, dst, f_recv.at[step, f, 0])
        return pltpu.make_async_remote_copy(
            src_ref=src, dst_ref=dst, send_sem=f_send.at[step, f, d],
            recv_sem=f_recv.at[step, f, d], device_id=(t, g), device_id_type=MESH,
        )

    def back(step, f, d):
        t = lax.rem(me + d, n)
        ys, xs = pl.ds(pl.multiple_of((me // tiles) * ROWS + ROWS, ROWS), ROWS), piece(me)[1]
        last = step == STEPS - 1
        low, count = (1 if last and f == 2 else 0), depth + (1 if last else 2)
        src = pout.at[f, pl.ds(t * depth + low, count)]
        dst = v_ext.at[3 * step + f, pl.ds(low, count), ys, xs]
        if d == 0:
            return pltpu.make_async_copy(src, dst, r_recv.at[step, f, 0])
        return pltpu.make_async_remote_copy(
            src_ref=src, dst_ref=dst, send_sem=r_send.at[step, f, d],
            recv_sem=r_recv.at[step, f, d], device_id=(t, g), device_id_type=MESH,
        )

    def start_all(make, step, f):
        for d in list(range(1, n)) + [0]:
            make(step, f, d).start()

    def wait_sent(make, step, f):
        for d in range(1, n):
            make(step, f, d).wait_send()

    def wait_got(make, step, f):
        make(step, f, 0).wait()
        for d in range(1, n):
            make(step, f, d).wait_recv()

    def share(step, d):
        return pltpu.make_async_remote_copy(
            src_ref=um.at[step, 0], dst_ref=um.at[step, d],
            send_sem=u_send.at[step, d], recv_sem=u_recv.at[step, d],
            device_id=(me, lax.rem(g + d, ng)), device_id_type=MESH,
        )

    def y_speed(step, f, i):
        return pltpu.make_async_remote_copy(
            src_ref=yg_send.at[step, f, i], dst_ref=yg_recv.at[step, f, i],
            send_sem=y_send.at[step, f, i], recv_sem=y_recv.at[step, f, i],
            device_id=(me, g + 1 - 2 * i), device_id_type=MESH,
        )

    has_next, has_last = g < ng - 1, g > 0
    planes = pl.ds(0, depth + 2)

    def stress_xy():
        def at(i, carry):
            shears(i + 1, ROWS, ROWS + side, (3,))
            return carry

        lax.fori_loop(0, depth, at, 0)

        @pl.when(g == ng - 1)
        def _():
            s_ext[3, planes, ROWS + side, :] = jnp.zeros((depth + 2, line), jnp.float32)

    def stress_xz():
        def at(i, carry):
            normals(i + 1, ROWS, side, (0,))
            shears(i + 1, ROWS, side, (4,))
            return carry

        lax.fori_loop(0, depth, at, 0)
        shears(depth + 1, ROWS, side, (4,))

    def stress_yz():
        def at(i, carry):
            normals(i + 1, 0, ROWS + side, (1,))
            shears(i + 1, ROWS, ROWS + side, (5,))
            return carry

        lax.fori_loop(0, depth, at, 0)
        shears(depth + 1, ROWS, side, (5,))

        @pl.when(g == 0)
        def _():
            s_ext[1, planes, ROWS - 1, :] = jnp.zeros((depth + 2, line), jnp.float32)

        @pl.when(g == ng - 1)
        def _():
            s_ext[5, planes, ROWS + side, :] = jnp.zeros((depth + 2, line), jnp.float32)

    def stress_zz():
        def at(i, carry):
            normals(i, ROWS, side, (2,))
            return carry

        lax.fori_loop(0, depth + 1, at, 0)

    def v_copy(f):
        return pltpu.make_async_copy(
            v_ext.at[3 * (STEPS - 1) + f, pl.ds(1, depth), inner, :], v_out.at[f], o_sem.at[f]
        )

    def out_copy(f):
        return pltpu.make_async_copy(
            s_ext.at[f, pl.ds(1, depth), inner, :], s_out.at[f], o_sem.at[3 + f]
        )

    def arrive(f, step):
        wait_got(back, step, f)
        yg_send[step, f, 0] = v_ext[3 * step + f, planes, ROWS + side - 1, :]
        yg_send[step, f, 1] = v_ext[3 * step + f, planes, ROWS, :]

        @pl.when(has_next)
        def _():
            y_speed(step, f, 0).start()

        @pl.when(has_last)
        def _():
            y_speed(step, f, 1).start()
        if step == STEPS - 1:
            v_copy(f).start()

    def edges(f, step):
        @pl.when(has_last)
        def _():
            y_speed(step, f, 0).wait_recv()
            v_ext[3 * step + f, planes, ROWS - 1, :] = yg_recv[step, f, 0]
            y_speed(step, f, 1).wait_send()

        @pl.when(has_next)
        def _():
            y_speed(step, f, 1).wait_recv()
            v_ext[3 * step + f, planes, ROWS + side, :] = yg_recv[step, f, 1]
            y_speed(step, f, 0).wait_send()

    for step in range(STEPS):
        if step > 0:
            for f in range(3):
                wait_sent(there, step - 1, f)
        if step > 0:
            stress_xz()
        lax.fori_loop(0, depth, speed_x, 0)
        start_all(there, step, 0)
        if step > 0:
            edges(2, step - 1)
            stress_yz()
        lax.fori_loop(0, depth, speed_y, 0)
        start_all(there, step, 1)
        if step > 0:
            stress_zz()
        lax.fori_loop(0, depth, speed_z, 0)
        flat = acc[2].reshape(depth * side, line)
        part = lax.dot_general(
            flat, in_cols, (((1,), (1,)), ((), ())),
            precision=lax.Precision.HIGHEST, preferred_element_type=jnp.float32,
        ).reshape(depth, side, LANES)
        um[step, 0, pl.ds(0, depth), :] = jnp.sum(part * in_rows[None], axis=1)
        um[step, 0, pl.ds(depth, depth), :] = w_ref[...]
        um[step, 0, pl.ds(2 * depth, ROWS), :] = imp_ref[...]
        for d in range(1, ng):
            share(step, d).start()
        for d in range(1, ng):
            share(step, d).wait()
        every = um[step, 0]
        for d in range(1, ng):
            every = every + um[step, d]
        w = every[depth : 2 * depth] if step == 0 else wbuf[...]
        force = every[2 * depth : 2 * depth + 1] * (w - every[0:depth] / FOOT)
        wbuf[...] = w - pier_gain * force
        spread = (force[:, None, :] * in_rows[None]).reshape(depth * side, LANES)
        pushed = jnp.dot(
            spread, in_cols, precision=lax.Precision.HIGHEST, preferred_element_type=jnp.float32
        )
        acc[2] = acc[2] + soil_gain * pushed.reshape(depth, side, line)
        start_all(there, step, 2)

        for f in range(3):
            wait_got(there, step, f)
            if step > 0:
                wait_sent(back, step - 1, f)
            full = jnp.concatenate([pin[f, :, y, :] for y in range(ROWS)], axis=1)
            damped = jnp.dot(
                damp_ref[...], full, precision=lax.Precision.HIGHEST,
                preferred_element_type=jnp.float32,
            )
            for y in range(ROWS):
                pout[f, pl.ds(1, n * depth), y, :] = damped[:, y * LANES : (y + 1) * LANES]
            start_all(back, step, f)
        base[0] = 3 * step
        arrive(0, step)
        arrive(1, step)
        edges(0, step)
        edges(1, step)
        if step < STEPS - 1:
            stress_xy()
            arrive(2, step)
        else:
            def last_xy(i, carry):
                shears(i + 1, ROWS, side, (3,))
                return carry

            def last_rest(i, carry):
                normals(i + 1, ROWS, side)
                shears(i + 1, ROWS, side, (4,))
                return carry

            def last_yz(i, carry):
                shears(i + 1, ROWS, side, (5,))
                return carry

            lax.fori_loop(0, depth, last_xy, 0)
            out_copy(3).start()
            arrive(2, step)
            lax.fori_loop(0, depth, last_rest, 0)
            for f in (0, 1, 2, 4):
                out_copy(f).start()
            edges(2, step)
            lax.fori_loop(0, depth, last_yz, 0)
            out_copy(5).start()

    w_out[...] = wbuf[...]
    for f in range(3):
        wait_sent(there, STEPS - 1, f)
        wait_sent(back, STEPS - 1, f)
    for f in range(3):
        v_copy(f).wait()
    for f in range(6):
        out_copy(f).wait()


def fused_body(
    n, ng, velocity, stress, pier_velocity, buoyancy, layer, lame_table, shear_table, relax_table,
    impedance, footprint, damp_inverse,
):
    depth, side, line = buoyancy.shape
    own = pier_velocity.shape[1]
    g = lax.axis_index("gy")
    w_all = lax.dynamic_update_slice(
        jnp.zeros((depth, LANES), jnp.float32), pier_velocity, (0, g * own)
    )
    imp = lax.dynamic_update_slice(
        jnp.zeros((ROWS, LANES), jnp.float32),
        jnp.broadcast_to(impedance[None, :], (ROWS, own)), (0, g * own)
    )
    f32 = jnp.float32
    hbm = pl.BlockSpec(memory_space=pl.ANY)
    vmem = pl.BlockSpec(memory_space=pltpu.VMEM)
    smem = pl.BlockSpec(memory_space=pltpu.SMEM)
    dma = pltpu.SemaphoreType.DMA
    tall = side + 2 * ROWS
    stage = 2 * depth + ROWS
    v, s, w = pl.pallas_call(
        functools.partial(fused, n, ng),
        out_shape=(
            jax.ShapeDtypeStruct(velocity.shape, f32),
            jax.ShapeDtypeStruct(stress.shape, f32),
            jax.ShapeDtypeStruct((depth, LANES), f32),
        ),
        in_specs=[hbm] * 3 + [smem] * 5 + [vmem] * 3,
        out_specs=(hbm, hbm, vmem),
        scratch_shapes=[
            pltpu.VMEM((3 * STEPS, depth + 2, tall, line), f32),
            pltpu.VMEM((6, depth + 2, tall, line), f32),
            pltpu.VMEM((depth, side, line), f32),
            pltpu.VMEM((3, depth + 2, ROWS, LANES), f32),
            pltpu.VMEM((3, depth, side, line), f32),
            pltpu.VMEM((3, n * depth, ROWS, LANES), f32),
            pltpu.VMEM((3, n * depth + 2, ROWS, LANES), f32),
            pltpu.VMEM((STEPS, ng, stage, LANES), f32),
            pltpu.VMEM((depth, LANES), f32),
            pltpu.VMEM((3, depth, line), f32),
            pltpu.VMEM((3, depth, line), f32),
            pltpu.VMEM((STEPS, 3, 2, depth + 2, line), f32),
            pltpu.VMEM((STEPS, 3, 2, depth + 2, line), f32),
            dma((10,)), dma((3,)), dma((3,)), dma((2,)), dma((2,)), dma((3,)), dma((3,)),
            dma((STEPS, 3, n)), dma((STEPS, 3, n)), dma((STEPS, 3, n)), dma((STEPS, 3, n)),
            dma((STEPS, ng)), dma((STEPS, ng)), dma((STEPS, 3, 2)), dma((STEPS, 3, 2)),
            dma((9,)),
        ],
        compiler_params=pltpu.CompilerParams(
            collective_id=0, has_side_effects=True, vmem_limit_bytes=60 * 1024 * 1024
        ),
    )(
        velocity, stress, buoyancy, layer, lame_table, shear_table, relax_table,
        footprint, w_all, imp, damp_inverse,
    )
    return v, s, lax.dynamic_slice(w, (0, g * own), (depth, own))


def whole_tiles(mesh, velocity, pier_velocity):
    n, ng = mesh.shape["gx"], mesh.shape["gy"]
    depth, side, line = velocity.shape[1] // n, velocity.shape[2] // ng, velocity.shape[3]
    return (
        line % LANES == 0
        and side % ROWS == 0
        and depth % ROWS == 0
        and (side // ROWS) * (line // LANES) == n
        and pier_velocity.shape[1] <= LANES
    )


def solution(mesh):
    placed = (
        P(None, "gx", "gy", None),
        P(None, "gx", "gy", None),
        P("gx", "gy"),
        P("gx", "gy", None),
        P("gx"),
        P(),
        P(),
        P(),
        P("gy"),
        P(),
        P(),
    )

    def run(*args):
        n, ng = mesh.shape["gx"], mesh.shape["gy"]
        if whole_tiles(mesh, args[0], args[2]):
            part = functools.partial(fused_body, n, ng)
        else:
            part = body
        return mapped(part)(*args)

    def mapped(part):
        return jax.shard_map(
            part,
            mesh=mesh,
            in_specs=placed,
            out_specs=(P(None, "gx", "gy", None), P(None, "gx", "gy", None), P("gx", "gy")),
            check_vma=False,
        )

    return run
```

profile of v0, /device:TPU:0, one launch (start us, length us, event | category | flops | bytes accessed | tf_op | source)
XLA Modules:
  0.0 105.1 jit_solution(16272519476949043363)
XLA Ops:
  0.6 0.7 broadcast_in_dim.14
  1.3 0.1 dynamic_update_slice.7.imp_ref
  1.4 0.0 copy-start.2
  1.4 0.8 copy.14
  2.2 0.1 dynamic_update_slice.6.w_ref
  2.3 0.0 copy-done.2
  2.3 0.0 copy-start.1
  2.3 0.6 copy-done.1
  2.9 96.1 %shard_map.130 = (f32[3,16,16,512]{3,2,1,0:T(8,128)}, f32[6,16,16,512]{3,2,1,0:T(8,128)}, f32[16,128]{1,0:T(8,128)}) custom-call(f32[3,16,16,512]{3,2,1,0:T(8,128)} %v_hbm.1, f32[6,16,16,512]{3,2,1,0:T(8,128)} %s_hbm.1, f32[16,16,512]{2,1,0:T(8,128)} %b_hbm.1, s32[16]{0:T(128)} %layer_ref.1, f32[8]{0:T(128)} %lame_ref.1, f32[8]{0:T(128)} %shear_ref.1, ...), custom_call_target="tpu_custom_call" | custom-call | tf_op jit(solution)/shard_map/pallas_call | solution.py:669
  99.1 0.0 copy-start
  99.1 0.9 constant_dynamic-slice_fusion
  100.0 0.7 copy.15
  100.6 2.8 %copy.20 = f32[3,16,16,512]{3,2,1,0:T(8,128)} copy(f32[3,16,16,512]{3,2,1,0:T(8,128)} %get-tuple-element.15) | data formatting | bytes 3145728
  103.4 0.0 copy-done
  103.4 1.7 %copy.21 = f32[6,16,16,512]{3,2,1,0:T(8,128)} copy(f32[6,16,16,512]{3,2,1,0:T(8,128)S(1)} %copy-done) | data formatting | bytes 6291456
  (2 shorter events, 0.0 us)
Async XLA Ops:
  1.4 0.9 copy-start.2
  2.3 0.6 copy-start.1
  99.1 4.4 %copy-start = (f32[6,16,16,512]{3,2,1,0:T(8,128)S(1)}, f32[6,16,16,512]{3,2,1,0:T(8,128)}, u32[]{:S(2)}) copy-start(f32[6,16,16,512]{3,2,1,0:T(8,128)} %get-tuple-element.16) | copy-start | bytes 9437188
where the time goes:
time: 105 us
  Pallas kernels  96.1 us (92%)
  local copies, waits for them, and re-layouts  8.24 us (8%)
    pallas_call x1, Pallas kernels, fused_body(): pl.pallas_call(functools.partial(fused, n, ng), out_shape=(jax.ShapeDtype...  96.1 us
    unnamed x10, local copies, waits for them, and re-layouts  6.45 us

commit v1 on v0

--- a/solution.py
+++ b/solution.py
@@ -190,7 +190,7 @@
 def fused(
     n, ng, v_hbm, s_hbm, b_hbm, layer_ref, lame_ref, shear_ref, relax_ref, foot_ref, w_ref, imp_ref, damp_ref,
     v_out, s_out, w_out,
-    v_ext, s_ext, buoy, coef, acc, pin, pout, um, wbuf, sg_send, sg_recv, yg_send, yg_recv,
+    v_ext, s_ext, buoy, coef, acc, pin, pout, um, wbuf, square, sg_send, sg_recv, yg_send, yg_recv,
     load_sem, zs_send, zs_recv, cf_send, cf_recv, ys_send, ys_recv,
     f_send, f_recv, r_send, r_recv, u_send, u_recv, y_send, y_recv, o_sem,
 ):
@@ -353,6 +353,19 @@
         return ref[f, k, pl.ds(begin + shift, side if rows is None else rows), :]
 
     base = [0]
+
+    def own_w():
+        own = w_ref.shape[0]
+        square[...] = jnp.zeros((LANES, LANES), jnp.float32)
+        square[pl.ds(0, own), pl.ds(0, depth)] = w_ref[...]
+        return pltpu.roll(jnp.transpose(square[...])[0:depth], g * own, 1)
+
+    def own_impedance():
+        lane = lax.broadcasted_iota(jnp.int32, (ROWS, LANES), 1)
+        values = jnp.zeros((ROWS, LANES), jnp.float32)
+        for i in range(imp_ref.shape[0]):
+            values = jnp.where(lane == g * imp_ref.shape[0] + i, imp_ref[i], values)
+        return values
 
     def speed_x(i, carry):
         k = i + 1
@@ -418,10 +431,10 @@
         src = acc.at[f, :, ys, xs]
         dst = pin.at[f, pl.ds(me * depth, depth)]
         if d == 0:
-            return pltpu.make_async_copy(src, dst, f_recv.at[step, f, 0])
+            return pltpu.make_async_copy(src, dst, f_recv.at[step, f])
         return pltpu.make_async_remote_copy(
-            src_ref=src, dst_ref=dst, send_sem=f_send.at[step, f, d],
-            recv_sem=f_recv.at[step, f, d], device_id=(t, g), device_id_type=MESH,
+            src_ref=src, dst_ref=dst, send_sem=f_send.at[step, f],
+            recv_sem=f_recv.at[step, f], device_id=(t, g), device_id_type=MESH,
         )
 
     def back(step, f, d):
@@ -432,24 +445,35 @@
         src = pout.at[f, pl.ds(t * depth + low, count)]
         dst = v_ext.at[3 * step + f, pl.ds(low, count), ys, xs]
         if d == 0:
-            return pltpu.make_async_copy(src, dst, r_recv.at[step, f, 0])
+            return pltpu.make_async_copy(src, dst, r_recv.at[step, f])
         return pltpu.make_async_remote_copy(
-            src_ref=src, dst_ref=dst, send_sem=r_send.at[step, f, d],
-            recv_sem=r_recv.at[step, f, d], device_id=(t, g), device_id_type=MESH,
+            src_ref=src, dst_ref=dst, send_sem=r_send.at[step, f],
+            recv_sem=r_recv.at[step, f], device_id=(t, g), device_id_type=MESH,
         )
 
     def start_all(make, step, f):
         for d in list(range(1, n)) + [0]:
             make(step, f, d).start()
 
-    def wait_sent(make, step, f):
-        for d in range(1, n):
-            make(step, f, d).wait_send()
-
-    def wait_got(make, step, f):
-        make(step, f, 0).wait()
-        for d in range(1, n):
-            make(step, f, d).wait_recv()
+    def settle(ref, sem):
+        pltpu.make_async_copy(ref, ref, sem).wait()
+
+    def planes_back(step, f):
+        last = step == STEPS - 1
+        return (1 if last and f == 2 else 0), depth + (1 if last else 2)
+
+    def sent_there(step, f):
+        settle(pin.at[f, pl.ds(0, (n - 1) * depth)], f_send.at[step, f])
+
+    def got_there(step, f):
+        settle(pin.at[f], f_recv.at[step, f])
+
+    def sent_back(step, f):
+        settle(pout.at[f, pl.ds(0, (n - 1) * planes_back(step, f)[1])], r_send.at[step, f])
+
+    def got_back(step, f):
+        low, count = planes_back(step, f)
+        settle(v_ext.at[3 * step + f, pl.ds(low, count), inner, :], r_recv.at[step, f])
 
     def share(step, d):
         return pltpu.make_async_remote_copy(
@@ -523,7 +547,7 @@
         )
 
     def arrive(f, step):
-        wait_got(back, step, f)
+        got_back(step, f)
         yg_send[step, f, 0] = v_ext[3 * step + f, planes, ROWS + side - 1, :]
         yg_send[step, f, 1] = v_ext[3 * step + f, planes, ROWS, :]
 
@@ -553,7 +577,7 @@
     for step in range(STEPS):
         if step > 0:
             for f in range(3):
-                wait_sent(there, step - 1, f)
+                sent_there(step - 1, f)
         if step > 0:
             stress_xz()
         lax.fori_loop(0, depth, speed_x, 0)
@@ -572,8 +596,8 @@
             precision=lax.Precision.HIGHEST, preferred_element_type=jnp.float32,
         ).reshape(depth, side, LANES)
         um[step, 0, pl.ds(0, depth), :] = jnp.sum(part * in_rows[None], axis=1)
-        um[step, 0, pl.ds(depth, depth), :] = w_ref[...]
-        um[step, 0, pl.ds(2 * depth, ROWS), :] = imp_ref[...]
+        um[step, 0, pl.ds(depth, depth), :] = own_w()
+        um[step, 0, pl.ds(2 * depth, ROWS), :] = own_impedance()
         for d in range(1, ng):
             share(step, d).start()
         for d in range(1, ng):
@@ -592,9 +616,9 @@
         start_all(there, step, 2)
 
         for f in range(3):
-            wait_got(there, step, f)
+            got_there(step, f)
             if step > 0:
-                wait_sent(back, step - 1, f)
+                sent_back(step - 1, f)
             full = jnp.concatenate([pin[f, :, y, :] for y in range(ROWS)], axis=1)
             damped = jnp.dot(
                 damp_ref[...], full, precision=lax.Precision.HIGHEST,
@@ -635,14 +659,26 @@
             lax.fori_loop(0, depth, last_yz, 0)
             out_copy(5).start()
 
-    w_out[...] = wbuf[...]
+    own = w_ref.shape[0]
+    square[...] = jnp.zeros((LANES, LANES), jnp.float32)
+    square[pl.ds(0, depth), :] = pltpu.roll(wbuf[...], lax.rem(LANES - g * own, LANES), 1)
+    w_out[...] = jnp.transpose(square[...])[0:own, 0:depth]
     for f in range(3):
-        wait_sent(there, STEPS - 1, f)
-        wait_sent(back, STEPS - 1, f)
+        sent_there(STEPS - 1, f)
+        sent_back(STEPS - 1, f)
     for f in range(3):
         v_copy(f).wait()
     for f in range(6):
         out_copy(f).wait()
+
+
+def deliver(v_ref, s_ref, w_ref, v_out, s_out, w_out, sem):
+    pairs = ((v_ref, v_out), (s_ref, s_out), (w_ref, w_out))
+    copies = [pltpu.make_async_copy(a, b, sem.at[i]) for i, (a, b) in enumerate(pairs)]
+    for copy in copies:
+        copy.start()
+    for copy in copies:
+        copy.wait()
 
 
 def fused_body(
@@ -651,14 +687,6 @@
 ):
     depth, side, line = buoyancy.shape
     own = pier_velocity.shape[1]
-    g = lax.axis_index("gy")
-    w_all = lax.dynamic_update_slice(
-        jnp.zeros((depth, LANES), jnp.float32), pier_velocity, (0, g * own)
-    )
-    imp = lax.dynamic_update_slice(
-        jnp.zeros((ROWS, LANES), jnp.float32),
-        jnp.broadcast_to(impedance[None, :], (ROWS, own)), (0, g * own)
-    )
     f32 = jnp.float32
     hbm = pl.BlockSpec(memory_space=pl.ANY)
     vmem = pl.BlockSpec(memory_space=pltpu.VMEM)
@@ -671,9 +699,9 @@
         out_shape=(
             jax.ShapeDtypeStruct(velocity.shape, f32),
             jax.ShapeDtypeStruct(stress.shape, f32),
-            jax.ShapeDtypeStruct((depth, LANES), f32),
+            jax.ShapeDtypeStruct((own, depth), f32),
         ),
-        in_specs=[hbm] * 3 + [smem] * 5 + [vmem] * 3,
+        in_specs=[hbm] * 3 + [smem] * 5 + [vmem, smem, vmem],
         out_specs=(hbm, hbm, vmem),
         scratch_shapes=[
             pltpu.VMEM((3 * STEPS, depth + 2, tall, line), f32),
@@ -685,12 +713,13 @@
             pltpu.VMEM((3, n * depth + 2, ROWS, LANES), f32),
             pltpu.VMEM((STEPS, ng, stage, LANES), f32),
             pltpu.VMEM((depth, LANES), f32),
+            pltpu.VMEM((LANES, LANES), f32),
             pltpu.VMEM((3, depth, line), f32),
             pltpu.VMEM((3, depth, line), f32),
             pltpu.VMEM((STEPS, 3, 2, depth + 2, line), f32),
             pltpu.VMEM((STEPS, 3, 2, depth + 2, line), f32),
             dma((10,)), dma((3,)), dma((3,)), dma((2,)), dma((2,)), dma((3,)), dma((3,)),
-            dma((STEPS, 3, n)), dma((STEPS, 3, n)), dma((STEPS, 3, n)), dma((STEPS, 3, n)),
+            dma((STEPS, 3)), dma((STEPS, 3)), dma((STEPS, 3)), dma((STEPS, 3)),
             dma((STEPS, ng)), dma((STEPS, ng)), dma((STEPS, 3, 2)), dma((STEPS, 3, 2)),
             dma((9,)),
         ],
@@ -699,9 +728,16 @@
         ),
     )(
         velocity, stress, buoyancy, layer, lame_table, shear_table, relax_table,
-        footprint, w_all, imp, damp_inverse,
-    )
-    return v, s, lax.dynamic_slice(w, (0, g * own), (depth, own))
+        footprint, pier_velocity.T, impedance, damp_inverse,
+    )
+    v, s, w = pl.pallas_call(
+        deliver,
+        out_shape=tuple(jax.ShapeDtypeStruct(a.shape, f32) for a in (v, s, w)),
+        in_specs=[hbm] * 3,
+        out_specs=(hbm,) * 3,
+        scratch_shapes=[dma((3,))],
+    )(v, s, w)
+    return v, s, w.T
 
 
 def whole_tiles(mesh, velocity, pier_velocity):

time: 105 us -> 239 us (2.28)
  Pallas kernels: 96.1 us -> 239 us
  local copies, waits for them, and re-layouts: 8.24 us -> 0 us
    pallas_call x0 -> x1, Pallas kernels: none -> 144 us  [fused_body(): pl.pallas_call(deliver, out_shape=tuple((jax.ShapeDtypeStruct(a.shape, f3...]
    unnamed x10 -> x0, local copies, waits for them, and re-layouts: 6.45 us -> none
where the time goes in v1:
time: 239 us
  Pallas kernels  239 us (100%)
    pallas_call x1, Pallas kernels, fused_body(): pl.pallas_call(deliver, out_shape=tuple((jax.ShapeDtypeStruct(a.shape, f3...  144 us
    pallas_call x1, Pallas kernels, fused_body(): pl.pallas_call(functools.partial(fused, n, ng), out_shape=(jax.ShapeDtype...  94.5 us

profile of v1, /device:TPU:0, one launch (start us, length us, event | category | flops | bytes accessed | tf_op | source)
XLA Modules:
  0.0 239.3 jit_solution(16228004686252050281)
XLA Ops:
  0.6 94.5 %shard_map.130 = (f32[3,16,16,512]{3,2,1,0:T(8,128)}, f32[6,16,16,512]{3,2,1,0:T(8,128)}, f32[4,16]{1,0:T(4,128)}) custom-call(f32[3,16,16,512]{3,2,1,0:T(8,128)} %v_hbm.1, f32[6,16,16,512]{3,2,1,0:T(8,128)} %s_hbm.1, f32[16,16,512]{2,1,0:T(8,128)} %b_hbm.1, s32[16]{0:T(128)} %layer_ref.1, f32[8]{0:T(128)} %lame_ref.1, f32[8]{0:T(128)} %shear_ref.1, ...), custom_call_target="tpu_custom_call" | custom-call | tf_op jit(solution)/shard_map/pallas_call | solution.py:697
  95.1 144.1 %shard_map.131 = (f32[3,16,16,512]{3,2,1,0:T(8,128)}, f32[6,16,16,512]{3,2,1,0:T(8,128)}, f32[4,16]{1,0:T(4,128)}) custom-call(f32[3,16,16,512]{3,2,1,0:T(8,128)} %get-tuple-element.9.v_ref, f32[6,16,16,512]{3,2,1,0:T(8,128)} %get-tuple-element.10.s_ref, f32[4,16]{1,0:T(4,128)} %get-tuple-element.11.w_ref), custom_call_target="tpu_custom_call" | custom-call | tf_op jit(solution)/shard_map/pallas_call | solution.py:733

commit v2 on v1

--- a/solution.py
+++ b/solution.py
@@ -189,10 +189,10 @@
 
 def fused(
     n, ng, v_hbm, s_hbm, b_hbm, layer_ref, lame_ref, shear_ref, relax_ref, foot_ref, w_ref, imp_ref, damp_ref,
-    v_out, s_out, w_out,
-    v_ext, s_ext, buoy, coef, acc, pin, pout, um, wbuf, square, sg_send, sg_recv, yg_send, yg_recv,
+    v_ext, s_ext, w_out,
+    buoy, coef, acc, pin, pout, um, wbuf, square, sg_send, sg_recv, yg_send, yg_recv,
     load_sem, zs_send, zs_recv, cf_send, cf_recv, ys_send, ys_recv,
-    f_send, f_recv, r_send, r_recv, u_send, u_recv, y_send, y_recv, o_sem,
+    f_send, f_recv, r_send, r_recv, u_send, u_recv, y_send, y_recv,
 ):
     me = lax.axis_index("gx")
     g = lax.axis_index("gy")
@@ -536,16 +536,6 @@
 
         lax.fori_loop(0, depth + 1, at, 0)
 
-    def v_copy(f):
-        return pltpu.make_async_copy(
-            v_ext.at[3 * (STEPS - 1) + f, pl.ds(1, depth), inner, :], v_out.at[f], o_sem.at[f]
-        )
-
-    def out_copy(f):
-        return pltpu.make_async_copy(
-            s_ext.at[f, pl.ds(1, depth), inner, :], s_out.at[f], o_sem.at[3 + f]
-        )
-
     def arrive(f, step):
         got_back(step, f)
         yg_send[step, f, 0] = v_ext[3 * step + f, planes, ROWS + side - 1, :]
@@ -558,8 +548,6 @@
         @pl.when(has_last)
         def _():
             y_speed(step, f, 1).start()
-        if step == STEPS - 1:
-            v_copy(f).start()
 
     def edges(f, step):
         @pl.when(has_last)
@@ -650,14 +638,10 @@
                 return carry
 
             lax.fori_loop(0, depth, last_xy, 0)
-            out_copy(3).start()
             arrive(2, step)
             lax.fori_loop(0, depth, last_rest, 0)
-            for f in (0, 1, 2, 4):
-                out_copy(f).start()
             edges(2, step)
             lax.fori_loop(0, depth, last_yz, 0)
-            out_copy(5).start()
 
     own = w_ref.shape[0]
     square[...] = jnp.zeros((LANES, LANES), jnp.float32)
@@ -666,14 +650,16 @@
     for f in range(3):
         sent_there(STEPS - 1, f)
         sent_back(STEPS - 1, f)
-    for f in range(3):
-        v_copy(f).wait()
-    for f in range(6):
-        out_copy(f).wait()
 
 
 def deliver(v_ref, s_ref, w_ref, v_out, s_out, w_out, sem):
-    pairs = ((v_ref, v_out), (s_ref, s_out), (w_ref, w_out))
+    depth, side = v_out.shape[1:3]
+    inside = pl.ds(1, depth), pl.ds(ROWS, side)
+    pairs = (
+        (v_ref.at[(pl.ds(3 * (STEPS - 1), 3),) + inside], v_out),
+        (s_ref.at[(pl.ds(0, 6),) + inside], s_out),
+        (w_ref, w_out),
+    )
     copies = [pltpu.make_async_copy(a, b, sem.at[i]) for i, (a, b) in enumerate(pairs)]
     for copy in copies:
         copy.start()
@@ -688,7 +674,7 @@
     depth, side, line = buoyancy.shape
     own = pier_velocity.shape[1]
     f32 = jnp.float32
-    hbm = pl.BlockSpec(memory_space=pl.ANY)
+    hbm = pl.BlockSpec(memory_space=pltpu.HBM)
     vmem = pl.BlockSpec(memory_space=pltpu.VMEM)
     smem = pl.BlockSpec(memory_space=pltpu.SMEM)
     dma = pltpu.SemaphoreType.DMA
@@ -697,15 +683,13 @@
     v, s, w = pl.pallas_call(
         functools.partial(fused, n, ng),
         out_shape=(
-            jax.ShapeDtypeStruct(velocity.shape, f32),
-            jax.ShapeDtypeStruct(stress.shape, f32),
-            jax.ShapeDtypeStruct((own, depth), f32),
+            pltpu.VMEM((3 * STEPS, depth + 2, tall, line), f32),
+            pltpu.VMEM((6, depth + 2, tall, line), f32),
+            pltpu.VMEM((own, depth), f32),
         ),
         in_specs=[hbm] * 3 + [smem] * 5 + [vmem, smem, vmem],
-        out_specs=(hbm, hbm, vmem),
+        out_specs=(vmem, vmem, vmem),
         scratch_shapes=[
-            pltpu.VMEM((3 * STEPS, depth + 2, tall, line), f32),
-            pltpu.VMEM((6, depth + 2, tall, line), f32),
             pltpu.VMEM((depth, side, line), f32),
             pltpu.VMEM((3, depth + 2, ROWS, LANES), f32),
             pltpu.VMEM((3, depth, side, line), f32),
@@ -721,10 +705,9 @@
             dma((10,)), dma((3,)), dma((3,)), dma((2,)), dma((2,)), dma((3,)), dma((3,)),
             dma((STEPS, 3)), dma((STEPS, 3)), dma((STEPS, 3)), dma((STEPS, 3)),
             dma((STEPS, ng)), dma((STEPS, ng)), dma((STEPS, 3, 2)), dma((STEPS, 3, 2)),
-            dma((9,)),
         ],
         compiler_params=pltpu.CompilerParams(
-            collective_id=0, has_side_effects=True, vmem_limit_bytes=60 * 1024 * 1024
+            collective_id=0, has_side_effects=True, vmem_limit_bytes=48 * 1024 * 1024
         ),
     )(
         velocity, stress, buoyancy, layer, lame_table, shear_table, relax_table,
@@ -732,10 +715,13 @@
     )
     v, s, w = pl.pallas_call(
         deliver,
-        out_shape=tuple(jax.ShapeDtypeStruct(a.shape, f32) for a in (v, s, w)),
-        in_specs=[hbm] * 3,
+        out_shape=tuple(
+            jax.ShapeDtypeStruct(a, f32) for a in (velocity.shape, stress.shape, (own, depth))
+        ),
+        in_specs=[vmem] * 3,
         out_specs=(hbm,) * 3,
         scratch_shapes=[dma((3,))],
+        compiler_params=pltpu.CompilerParams(vmem_limit_bytes=8 * 1024 * 1024),
     )(v, s, w)
     return v, s, w.T
 

time: 239 us -> 96.3 us (0.40)
  Pallas kernels: 239 us -> 95.5 us
    pallas_call x2, Pallas kernels: 239 us -> 95.5 us  [the longest x1 93.2 us: fused_body(): pl.pallas_call(functools.partial(fused, n, ng), out_shape=(pltpu.VMEM((3...]
where the time goes in v2:
time: 96.3 us; the launch traced here: 96.1 us
  Pallas kernels  95.5 us (99%)
    pallas_call x1, Pallas kernels, fused_body(): pl.pallas_call(functools.partial(fused, n, ng), out_shape=(pltpu.VMEM((3...  93.2 us
    pallas_call x1, Pallas kernels, fused_body(): pl.pallas_call(deliver, out_shape=tuple((jax.ShapeDtypeStruct(a, f32) for...  2.21 us

profile of v2, /device:TPU:0, one launch (start us, length us, event | category | flops | bytes accessed | tf_op | source)
XLA Modules:
  0.0 96.1 jit_solution(11360040429793379278)
XLA Ops:
  0.6 93.2 %shard_map.130 = (f32[6,18,32,512]{3,2,1,0:T(8,128)S(1)}, f32[6,18,32,512]{3,2,1,0:T(8,128)S(1)}, f32[4,16]{1,0:T(4,128)S(1)}) custom-call(f32[3,16,16,512]{3,2,1,0:T(8,128)} %v_hbm.1, f32[6,16,16,512]{3,2,1,0:T(8,128)} %s_hbm.1, f32[16,16,512]{2,1,0:T(8,128)} %b_hbm.1, s32[16]{0:T(128)} %layer_ref.1, f32[8]{0:T(128)} %lame_ref.1, f32[8]{0:T(128)} %shear_ref.1, ...), custom_call_target="tpu_custom_call" | custom-call | tf_op jit(solution)/shard_map/pallas_call | solution.py:683
  93.9 2.2 %shard_map.131 = (f32[3,16,16,512]{3,2,1,0:T(8,128)}, f32[6,16,16,512]{3,2,1,0:T(8,128)}, f32[4,16]{1,0:T(4,128)}) custom-call(f32[6,18,32,512]{3,2,1,0:T(8,128)S(1)} %get-tuple-element.9.v_ref, f32[6,18,32,512]{3,2,1,0:T(8,128)S(1)} %get-tuple-element.10.s_ref, f32[4,16]{1,0:T(4,128)S(1)} %get-tuple-element.11.w_ref), custom_call_target="tpu_custom_call" | custom-call | tf_op jit(solution)/shard_map/pallas_call | solution.py:716

commit v3 on v2

v3 whole, which is shorter than its diff:
```python
import functools
import jax
import jax.numpy as jnp
from jax import lax
from jax.experimental import pallas as pl
from jax.experimental.pallas import tpu as pltpu
from jax.sharding import PartitionSpec as P

STEPS = 2
FOOT = 16


grid_ratio = 0.25
soil_gain = 0.2
pier_gain = 0.5


def extended(cells, sides, width):
    for axis, dim in sides:
        count = lax.axis_size(axis)
        ends = count - 1
        head = lax.slice_in_dim(cells, 0, width, axis=dim)
        tail = lax.slice_in_dim(cells, cells.shape[dim] - width, cells.shape[dim], axis=dim)
        cells = jnp.concatenate(
            [
                lax.ppermute(tail, axis, [(i, (i + 1) % count) for i in range(ends)]),
                cells,
                lax.ppermute(head, axis, [((i + 1) % count, i) for i in range(ends)]),
            ],
            axis=dim,
        )
    return cells


def forward_diff(padded, along):
    center = padded[1:-1, 1:-1, 1:-1]
    if along == 0:
        return padded[2:, 1:-1, 1:-1] - center
    if along == 1:
        return padded[1:-1, 2:, 1:-1] - center
    return padded[1:-1, 1:-1, 2:] - center


def backward_diff(padded, along):
    center = padded[1:-1, 1:-1, 1:-1]
    if along == 0:
        return center - padded[:-2, 1:-1, 1:-1]
    if along == 1:
        return center - padded[1:-1, :-2, 1:-1]
    return center - padded[1:-1, 1:-1, :-2]


def move_velocity(velocity, padded, buoyancy):
    scaled = grid_ratio * buoyancy
    first = velocity[0] + scaled * (
        backward_diff(padded[0], 2) + forward_diff(padded[3], 1) + forward_diff(padded[4], 0)
    )
    second = velocity[1] + scaled * (
        forward_diff(padded[3], 2) + backward_diff(padded[1], 1) + forward_diff(padded[5], 0)
    )
    third = velocity[2] + scaled * (
        forward_diff(padded[4], 2) + forward_diff(padded[5], 1) + backward_diff(padded[2], 0)
    )
    return jnp.stack([first, second, third])


def move_stress(stress, padded, lame_first, shear_mod, relax):
    strain_x = forward_diff(padded[0], 2)
    strain_y = forward_diff(padded[1], 1)
    strain_z = forward_diff(padded[2], 0)
    modulus = lame_first + 2.0 * shear_mod
    normal_x = relax * stress[0] + grid_ratio * (
        modulus * strain_x + lame_first * (strain_y + strain_z)
    )
    normal_y = relax * stress[1] + grid_ratio * (
        modulus * strain_y + lame_first * (strain_x + strain_z)
    )
    normal_z = relax * stress[2] + grid_ratio * (
        modulus * strain_z + lame_first * (strain_x + strain_y)
    )
    shear_xy = relax * stress[3] + grid_ratio * shear_mod * (
        backward_diff(padded[0], 1) + backward_diff(padded[1], 2)
    )
    shear_xz = relax * stress[4] + grid_ratio * shear_mod * (
        backward_diff(padded[0], 0) + backward_diff(padded[2], 2)
    )
    shear_yz = relax * stress[5] + grid_ratio * shear_mod * (
        backward_diff(padded[1], 0) + backward_diff(padded[2], 1)
    )
    return jnp.stack([normal_x, normal_y, normal_z, shear_xy, shear_xz, shear_yz])


def layer_values(layer, table):
    levels = jnp.arange(table.shape[0], dtype=jnp.int32)
    onehot = (layer[:, None] == levels[None, :]).astype(table.dtype)
    return jnp.sum(onehot * table[None, :], axis=1)[:, None, None]


def with_faces(fields):
    padded = extended(fields, (("gx", 1), ("gy", 2)), 1)
    return jnp.pad(padded, ((0, 0), (0, 0), (0, 0), (1, 1)))


def footprint_matches(cell_ids, footprint):
    piers = footprint.shape[0]
    equal = (cell_ids[:, None] == footprint.reshape(-1)[None, :]).astype(jnp.float32)
    return jnp.sum(equal.reshape(cell_ids.shape[0], piers, FOOT), axis=2)


def damp_columns(velocity, inverse):
    pencils = lax.all_to_all(velocity, "gx", split_axis=3, concat_axis=1, tiled=True)
    shape = pencils.shape
    flat = pencils.reshape(shape[0], shape[1], shape[2] * shape[3])
    damped = jnp.einsum("zk,fkm->fzm", inverse, flat, precision=lax.Precision.HIGHEST).reshape(
        shape
    )
    return lax.all_to_all(damped, "gx", split_axis=1, concat_axis=3, tiled=True)


def body(
    velocity,
    stress,
    pier_velocity,
    buoyancy,
    layer,
    lame_table,
    shear_table,
    relax_table,
    impedance,
    footprint,
    damp_inverse,
):
    depth_cells, side_cells, line_cells = (velocity.shape[1], velocity.shape[2], velocity.shape[3])
    own_piers = pier_velocity.shape[1]
    lame_first = layer_values(layer, lame_table)
    shear_mod = layer_values(layer, shear_table)
    relax = layer_values(layer, relax_table)
    row_start = lax.axis_index("gy") * side_cells
    cell_ids = row_start * line_cells + jnp.arange(side_cells * line_cells, dtype=jnp.int32)
    selector = footprint_matches(cell_ids, footprint)
    own_foot = lax.dynamic_slice_in_dim(footprint, lax.axis_index("gy") * own_piers, own_piers, 0)
    for time_step in range(STEPS):
        padded = with_faces(stress)
        velocity = move_velocity(velocity, padded, buoyancy)
        vertical = velocity[2].reshape(depth_cells, side_cells * line_cells)
        piece = lax.all_gather(velocity[2], "gy", axis=1, tiled=True)
        count = piece.shape[1]
        piece_ids = jnp.arange(count * line_cells, dtype=jnp.int32)
        picks = footprint_matches(piece_ids, own_foot)
        flat = piece.reshape(depth_cells, count * line_cells)
        summed = jnp.dot(
            flat, picks, precision=lax.Precision.HIGHEST, preferred_element_type=jnp.float32
        )
        mean_speed = summed / FOOT
        force = impedance[None, :] * (pier_velocity - mean_speed)
        pier_velocity = pier_velocity - pier_gain * force
        all_force = lax.all_gather(force, "gy", axis=1, tiled=True)
        pushed = jnp.dot(
            all_force,
            selector.T,
            precision=lax.Precision.HIGHEST,
            preferred_element_type=jnp.float32,
        )
        vertical = vertical + soil_gain * pushed
        velocity = jnp.stack(
            [velocity[0], velocity[1], vertical.reshape(depth_cells, side_cells, line_cells)]
        )
        velocity = damp_columns(velocity, damp_inverse)
        padded = with_faces(velocity)
        stress = move_stress(stress, padded, lame_first, shear_mod, relax)
    return (velocity, stress, pier_velocity)


SIDE = 4
LANES = 128
ROWS = 8
BLOCK = 4
MESH = pl.DeviceIdType.MESH
Z_GHOSTS = ((2, -1), (4, 1), (5, 1))
Y_GHOSTS = ((1, -1), (3, 1), (5, 1))


def fused(
    n, ng, v_hbm, s_hbm, b_hbm, layer_ref, lame_ref, shear_ref, relax_ref, foot_ref, w_ref, imp_ref, damp_ref,
    v_ext, s_ext, w_out,
    buoy, coef, acc, pin, pout, um, fall, wbuf, square, part, rows_of, cols_t, cols_of, spread, damp_cat, damp_own,
    load_sem, zs_send, zs_recv, cf_send, cf_recv, ys_send, ys_recv,
    f_send, f_recv, r_send, r_recv, u_send, u_recv, p_send, p_recv, y_send, y_recv,
):
    me = lax.axis_index("gx")
    g = lax.axis_index("gy")
    depth, side, line = buoy.shape
    tiles = line // LANES
    share_rows = side // n
    inner = pl.ds(ROWS, side)
    own = w_ref.shape[0]
    f32, bf16 = jnp.float32, jnp.bfloat16
    above, below = ROWS - 1, ROWS + side

    def lanes(c):
        return pl.ds(c * LANES, LANES)

    def settle(ref, sem):
        pltpu.make_async_copy(ref, ref, sem).wait()

    loads = []
    for c in range(tiles):
        loads.append((
            pltpu.make_async_copy(
                s_hbm.at[:, :, :, lanes(c)], s_ext.at[:, pl.ds(1, depth), inner, lanes(c)], load_sem.at[c]
            ),
            pltpu.make_async_copy(b_hbm.at[:, :, lanes(c)], buoy.at[:, :, lanes(c)], load_sem.at[tiles + c]),
            pltpu.make_async_copy(
                v_hbm.at[:, :, :, lanes(c)], v_ext.at[pl.ds(0, 3), pl.ds(1, depth), inner, lanes(c)],
                load_sem.at[2 * tiles + c],
            ),
        ))
        for copy in loads[c]:
            copy.start()

    plane = jnp.zeros((side, line), f32)
    for f, way in Z_GHOSTS:
        s_ext[f, 0 if way < 0 else depth + 1, inner, :] = plane
    edge = jnp.zeros((depth + 2, line), f32)
    for f, way in Y_GHOSTS:
        s_ext[f, :, above if way < 0 else below, :] = edge
    for f in range(3 * STEPS):
        v_ext[f, :, above, :] = edge
        v_ext[f, :, below, :] = edge
    for k in range(depth):
        for c, (table, scale) in enumerate(((lame_ref, grid_ratio), (shear_ref, grid_ratio), (relax_ref, 1.0))):
            coef[c, k + 1] = jnp.full((side, LANES), scale * table[layer_ref[k]], f32)
    for c in range(3):
        coef[c, 0] = jnp.zeros((side, LANES), f32)
        coef[c, depth + 1] = jnp.zeros((side, LANES), f32)
        pout[c, 0] = jnp.zeros((ROWS, LANES), f32)
        pout[c, n * depth + 1] = jnp.zeros((ROWS, LANES), f32)

    barrier = pltpu.get_barrier_semaphore()
    for d in range(1, n):
        pl.semaphore_signal(
            barrier, inc=1, device_id=(lax.rem(me + d, n), g), device_id_type=MESH
        )
    for d in range(1, ng):
        pl.semaphore_signal(
            barrier, inc=1, device_id=(me, lax.rem(g + d, ng)), device_id_type=MESH
        )
    pl.semaphore_wait(barrier, n - 1 + ng - 1)

    def z_copy(i):
        f, way = Z_GHOSTS[i]
        return pltpu.make_async_remote_copy(
            src_ref=s_hbm.at[f, depth - 1 if way < 0 else 0],
            dst_ref=s_ext.at[f, 0 if way < 0 else depth + 1, inner, :],
            send_sem=zs_send.at[i], recv_sem=zs_recv.at[i],
            device_id=(me - way, g), device_id_type=MESH,
        )

    def c_copy(way):
        i = (way + 1) // 2
        return pltpu.make_async_remote_copy(
            src_ref=coef.at[:, depth if way < 0 else 1],
            dst_ref=coef.at[:, 0 if way < 0 else depth + 1],
            send_sem=cf_send.at[i], recv_sem=cf_recv.at[i],
            device_id=(me - way, g), device_id_type=MESH,
        )

    def y_stress(i):
        f, way = Y_GHOSTS[i]
        return pltpu.make_async_remote_copy(
            src_ref=s_hbm.at[f, :, pl.ds(side - 1 if way < 0 else 0, 1), :],
            dst_ref=s_ext.at[f, pl.ds(1, depth), pl.ds(above if way < 0 else below, 1), :],
            send_sem=ys_send.at[i], recv_sem=ys_recv.at[i],
            device_id=(me, g - way), device_id_type=MESH,
        )

    not_ends = {
        -1: (me > 0, me < n - 1, g > 0, g < ng - 1),
        1: (me < n - 1, me > 0, g < ng - 1, g > 0),
    }
    ghosts = [(z_copy, i, not_ends[way][0:2]) for i, (f, way) in enumerate(Z_GHOSTS)]
    ghosts += [(y_stress, i, not_ends[way][2:4]) for i, (f, way) in enumerate(Y_GHOSTS)]
    ghosts += [(c_copy, way, not_ends[way][0:2]) for way in (-1, 1)]
    for make, i, (gets, sends) in ghosts:
        @pl.when(sends)
        def _(make=make, i=i):
            make(i).start()

    ids = lax.broadcasted_iota(jnp.int32, (side, LANES), 0) + g * side
    lane_id = lax.broadcasted_iota(jnp.int32, (2 * LANES, LANES), 1)
    row_id = lax.rem(lax.broadcasted_iota(jnp.int32, (2 * LANES, LANES), 0), LANES)
    first = jnp.full((1, LANES), -64, jnp.int32)
    begin_lane = jnp.full((1, LANES), -64, jnp.int32)
    begin_row = jnp.full((2 * LANES, LANES), -64, jnp.int32)
    for p in range(foot_ref.shape[0]):
        first = jnp.where(lane_id[0:1] == p, foot_ref[p, 0] // line, first)
        begin_lane = jnp.where(lane_id[0:1] == p, foot_ref[p, 0] % line, begin_lane)
        begin_row = jnp.where(row_id == p, foot_ref[p, 0] % line, begin_row)
    rows_of[...] = jnp.where((ids >= first) & (ids < first + SIDE), 1.0, 0.0)
    for c in range(tiles):
        at = row_id + c * LANES
        cols_t[c] = jnp.where((at >= begin_lane) & (at < begin_lane + SIDE), 1.0, 0.0).astype(bf16)
        at = lane_id + c * LANES
        cols_of[:, lanes(c)] = jnp.where((at >= begin_row) & (at < begin_row + SIDE), 1.0, 0.0).astype(bf16)

    def halves(a):
        high = a.astype(bf16)
        return high, (a - high.astype(f32)).astype(bf16)

    high, low = halves(damp_ref[...])
    damp_cat[...] = jnp.concatenate([high, high, low], axis=1)
    damp_own[...] = jnp.zeros_like(damp_own)
    damp_own[pl.ds(1, depth), :] = damp_ref[pl.ds(pl.multiple_of(me * depth, depth), depth), :]

    @pl.when(me > 0)
    def _():
        damp_own[pl.ds(0, 1), :] = damp_ref[pl.ds(me * depth - 1, 1), :]

    @pl.when(me < n - 1)
    def _():
        damp_own[pl.ds(depth + 1, 1), :] = damp_ref[pl.ds((me + 1) * depth, 1), :]

    square[...] = jnp.zeros((LANES, LANES), f32)
    square[pl.ds(0, own), pl.ds(0, depth)] = w_ref[...]
    wbuf[...] = pltpu.roll(jnp.transpose(square[...])[0:depth], g * own, 1)
    impedance = jnp.zeros((ROWS, LANES), f32)
    for i in range(imp_ref.shape[0]):
        impedance = jnp.where(lane_id[0:ROWS] == g * own + i, imp_ref[i], impedance)

    def look(ref, f, k, count, c, dy=0, dz=0):
        return ref[f, pl.ds(k + dz, count), pl.ds(ROWS + dy, side), lanes(c)].reshape(count * side, LANES)

    def row(ref, f, c, at, dz=0):
        return ref[f, pl.ds(1 + dz, depth), at, lanes(c)]

    def ahead(get, c):
        cell = get(c)
        lane = lax.broadcasted_iota(jnp.int32, cell.shape, 1)
        other = 0.0 if c == tiles - 1 else pltpu.roll(get(c + 1), LANES - 1, 1)
        return jnp.where(lane == LANES - 1, other, pltpu.roll(cell, LANES - 1, 1))

    def behind(get, c):
        cell = get(c)
        lane = lax.broadcasted_iota(jnp.int32, cell.shape, 1)
        other = 0.0 if c == 0 else pltpu.roll(get(c - 1), 1, 1)
        return jnp.where(lane == 0, other, pltpu.roll(cell, 1, 1))

    def blocks(run, size=BLOCK):
        def at(i, carry):
            run(1 + i * size, size)
            return carry

        lax.fori_loop(0, depth // size, at, 0)

    def moduli(k, count):
        return [coef[c, pl.ds(k, count)].reshape(count * side, LANES) for c in range(3)]

    def put(ref, f, k, count, c, value):
        ref[f, pl.ds(k, count), inner, lanes(c)] = value.reshape(count, side, LANES)

    def speeds(step, c):
        base = 3 * (step - 1) if step > 0 else 0

        def run(k, count):
            at = functools.partial(look, s_ext)
            scaled = grid_ratio * buoy[pl.ds(k - 1, count), :, lanes(c)].reshape(count * side, LANES)
            xx, yy, zz, xy, xz, yz = (at(f, k, count, c) for f in range(6))
            total = (xx - behind(lambda c: at(0, k, count, c), c)) + (at(3, k, count, c, 1) - xy)
            total = total + (at(4, k, count, c, 0, 1) - xz)
            values = [total]
            total = (ahead(lambda c: at(3, k, count, c), c) - xy) + (yy - at(1, k, count, c, -1))
            values.append(total + (at(5, k, count, c, 0, 1) - yz))
            total = (ahead(lambda c: at(4, k, count, c), c) - xz) + (at(5, k, count, c, 1) - yz)
            values.append(total + (zz - at(2, k, count, c, 0, -1)))
            for f in range(3):
                value = look(v_ext, base + f, k, count, c) + scaled * values[f]
                acc[f, pl.ds(k - 1, count), :, lanes(c)] = value.reshape(count, side, LANES)

        blocks(run)
        high, low = halves(acc[2, :, :, lanes(c)].reshape(depth * side, LANES))
        term = jnp.dot(jnp.concatenate([high, low], axis=1), cols_t[c], preferred_element_type=f32)
        part[...] = term if c == 0 else part[...] + term

    def shears(step, c, with_ghosts, which=(3, 4, 5)):
        at = functools.partial(look, v_ext)
        x, y, z = (3 * step + f for f in range(3))

        def run(k, count, which=which):
            lame, shear, relax = moduli(k, count)
            for f in which:
                if f == 3:
                    strain = (at(x, k, count, c) - at(x, k, count, c, -1)) + (
                        at(y, k, count, c) - behind(lambda c: at(y, k, count, c), c)
                    )
                elif f == 4:
                    strain = (at(x, k, count, c) - at(x, k, count, c, 0, -1)) + (
                        at(z, k, count, c) - behind(lambda c: at(z, k, count, c), c)
                    )
                else:
                    strain = (at(y, k, count, c) - at(y, k, count, c, 0, -1)) + (
                        at(z, k, count, c) - at(z, k, count, c, -1)
                    )
                put(s_ext, f, k, count, c, relax * look(s_ext, f, k, count, c) + shear * strain)

        blocks(run)
        if with_ghosts:
            run(depth + 1, 1, (4, 5))
            shear, relax = (coef[i, pl.ds(1, depth), 0, :] for i in (1, 2))
            y_at = functools.partial(row, v_ext, y, at=below)
            strain = (row(v_ext, x, c, below) - row(v_ext, x, c, below - 1)) + (
                y_at(c) - behind(lambda c: y_at(c), c)
            )
            xy = relax * row(s_ext, 3, c, below) + shear * strain
            strain = (y_at(c) - y_at(c, dz=-1)) + (row(v_ext, z, c, below) - row(v_ext, z, c, below - 1))
            yz = relax * row(s_ext, 5, c, below) + shear * strain
            s_ext[3, pl.ds(1, depth), below, lanes(c)] = jnp.where(g == ng - 1, 0.0, xy)
            s_ext[5, pl.ds(1, depth), below, lanes(c)] = jnp.where(g == ng - 1, 0.0, yz)

    def normals(step, c, with_ghosts):
        at = functools.partial(look, v_ext)
        x, y, z = (3 * step + f for f in range(3))

        def run(k, count, which=(0, 1, 2)):
            lame, shear, relax = moduli(k, count)
            ex = ahead(lambda c: at(x, k, count, c), c) - at(x, k, count, c)
            ey = at(y, k, count, c, 1) - at(y, k, count, c)
            ez = at(z, k, count, c, 0, 1) - at(z, k, count, c)
            trace = lame * ((ex + ey) + ez)
            twice = shear + shear
            for f in which:
                value = relax * look(s_ext, f, k, count, c) + (twice * (ex, ey, ez)[f] + trace)
                put(s_ext, f, k, count, c, value)

        blocks(run)
        if with_ghosts:
            run(0, 1, (2,))
            lame, shear, relax = (coef[i, pl.ds(1, depth), 0, :] for i in range(3))
            x_at = functools.partial(row, v_ext, x, at=above)
            ex = ahead(lambda c: x_at(c), c) - x_at(c)
            ey = row(v_ext, y, c, ROWS) - row(v_ext, y, c, above)
            ez = row(v_ext, z, c, above, 1) - row(v_ext, z, c, above)
            yy = relax * row(s_ext, 1, c, above) + ((shear + shear) * ey + lame * ((ex + ey) + ez))
            s_ext[1, pl.ds(1, depth), above, lanes(c)] = jnp.where(g == 0, 0.0, yy)

    def mine(t):
        return pl.ds(t * share_rows, share_rows)

    def there(step, c, d):
        t = lax.rem(me + d, n)
        src = acc.at[:, :, mine(t), lanes(c)]
        dst = pin.at[:, pl.ds(me * depth, depth), mine(c), :]
        if d == 0:
            return pltpu.make_async_copy(src, dst, f_recv.at[step, c])
        return pltpu.make_async_remote_copy(
            src_ref=src, dst_ref=dst, send_sem=f_send.at[step, c],
            recv_sem=f_recv.at[step, c], device_id=(t, g), device_id_type=MESH,
        )

    def back(step, c, d):
        t = lax.rem(me + d, n)
        pieces = ((0, 3, 0, depth + 2),)
        if step == STEPS - 1:
            pieces = ((0, 2, 0, depth + 1), (2, 1, 1, depth + 1))
        copies = []
        for f, fields, low, count in pieces:
            src = pout.at[pl.ds(f, fields), pl.ds(t * depth + low, count), mine(c), :]
            dst = v_ext.at[
                pl.ds(3 * step + f, fields), pl.ds(low, count), pl.ds(ROWS + me * share_rows, share_rows), lanes(c)
            ]
            if d == 0:
                copies.append(pltpu.make_async_copy(src, dst, r_recv.at[step, c]))
            else:
                copies.append(pltpu.make_async_remote_copy(
                    src_ref=src, dst_ref=dst, send_sem=r_send.at[step, c],
                    recv_sem=r_recv.at[step, c], device_id=(t, g), device_id_type=MESH,
                ))
        return copies

    def count_back(step):
        return depth + (1 if step == STEPS - 1 else 2)

    def start_there(step, c):
        for d in list(range(1, n)) + [0]:
            there(step, c, d).start()

    def start_back(step, c):
        for d in list(range(1, n)) + [0]:
            for copy in back(step, c, d):
                copy.start()

    def sent_there(step, c):
        settle(pin.at[:, pl.ds(0, (n - 1) * depth), mine(c), :], f_send.at[step, c])

    def got_there(step, c):
        settle(pin.at[:, :, mine(c), :], f_recv.at[step, c])

    def sent_back(step, c):
        settle(pout.at[:, pl.ds(0, (n - 1) * count_back(step)), mine(c), :], r_send.at[step, c])

    def got_back(step, c):
        settle(
            v_ext.at[pl.ds(3 * step, 3), pl.ds(0, count_back(step)), inner, lanes(c)], r_recv.at[step, c]
        )

    def damp(step, c):
        got_there(step, c)
        if step > 0:
            sent_back(step - 1, c)
        for f in range(3):
            terms = []
            for r in range(share_rows):
                high, low = halves(pin[f, :, share_rows * c + r, :])
                terms.append(jnp.concatenate([high, low, high], axis=0))
            damped = jnp.dot(damp_cat[...], jnp.concatenate(terms, axis=1), preferred_element_type=f32)
            for r in range(share_rows):
                pout[f, pl.ds(1, n * depth), share_rows * c + r, :] = damped[:, r * LANES : (r + 1) * LANES]
        start_back(step, c)

    def share(step, d):
        return pltpu.make_async_remote_copy(
            src_ref=um.at[step, 0], dst_ref=um.at[step, d],
            send_sem=u_send.at[step], recv_sem=u_recv.at[step],
            device_id=(me, lax.rem(g + d, ng)), device_id_type=MESH,
        )

    def forces(step, d):
        block = pl.ds(pl.multiple_of(me * depth, depth), depth)
        return pltpu.make_async_remote_copy(
            src_ref=fall.at[step, block], dst_ref=fall.at[step, block],
            send_sem=p_send.at[step], recv_sem=p_recv.at[step],
            device_id=(lax.rem(me + d, n), g), device_id_type=MESH,
        )

    def pier_means(step):
        masked = part[...].reshape(depth, side, LANES) * rows_of[...][None]
        um[step, 0, pl.ds(0, depth), :] = jnp.sum(masked, axis=1)
        um[step, 0, pl.ds(depth, depth), :] = wbuf[...]
        um[step, 0, pl.ds(2 * depth, ROWS), :] = impedance
        for d in range(1, ng):
            share(step, d).start()

    def pier_forces(step):
        settle(um.at[step, pl.ds(1, ng - 1)], u_recv.at[step])
        settle(um.at[step, pl.ds(1, ng - 1)], u_send.at[step])
        every = um[step, 0]
        for d in range(1, ng):
            every = every + um[step, d]
        w = every[depth : 2 * depth] if step == 0 else wbuf[...]
        force = every[2 * depth : 2 * depth + 1] * (w - every[0:depth] / FOOT)
        wbuf[...] = w - pier_gain * force
        fall[step, pl.ds(pl.multiple_of(me * depth, depth), depth), :] = soil_gain * force
        for d in range(1, n):
            forces(step, d).start()

    def pier_spread(step):
        settle(fall.at[step, pl.ds(0, (n - 1) * depth)], p_recv.at[step])
        settle(fall.at[step, pl.ds(0, (n - 1) * depth)], p_send.at[step])
        pushed = jnp.dot(
            damp_own[...], fall[step], precision=lax.Precision.HIGHEST, preferred_element_type=f32
        )[0 : depth + 2]
        wide = (pushed[:, None, :] * rows_of[...][None]).reshape((depth + 2) * side, LANES)
        spread[...] = jnp.concatenate(halves(wide), axis=1)

    def y_speed(step, c, i):
        low, count = (0, depth + 2) if step < STEPS - 1 else (1, depth)
        fields, planes = pl.ds(3 * step, 3), pl.ds(low, count)
        return pltpu.make_async_remote_copy(
            src_ref=v_ext.at[fields, planes, pl.ds(below - 1 if i == 0 else ROWS, 1), lanes(c)],
            dst_ref=v_ext.at[fields, planes, pl.ds(above if i == 0 else below, 1), lanes(c)],
            send_sem=y_send.at[step, c, i], recv_sem=y_recv.at[step, c, i],
            device_id=(me, g + 1 - 2 * i), device_id_type=MESH,
        )

    has_next, has_last = g < ng - 1, g > 0

    def arrive(step, c):
        got_back(step, c)
        low, count = (0, depth + 2) if step < STEPS - 1 else (1, depth + 1)
        term = jnp.dot(
            spread[pl.ds(low * side, count * side), :], cols_of[:, lanes(c)], preferred_element_type=f32
        )
        put(v_ext, 3 * step + 2, low, count, c, look(v_ext, 3 * step + 2, low, count, c) + term)

        @pl.when(has_next)
        def _():
            y_speed(step, c, 0).start()

        @pl.when(has_last)
        def _():
            y_speed(step, c, 1).start()

    def edges(step, c):
        @pl.when(has_last)
        def _():
            y_speed(step, c, 0).wait_recv()
            y_speed(step, c, 1).wait_send()

        @pl.when(has_next)
        def _():
            y_speed(step, c, 1).wait_recv()
            y_speed(step, c, 0).wait_send()

    def load(c):
        for copy in loads[c]:
            copy.wait()

    for make, i, (gets, sends) in ghosts:
        @pl.when(gets)
        def _(make=make, i=i):
            make(i).wait_recv()

        @pl.when(sends)
        def _(make=make, i=i):
            make(i).wait_send()

    last = tiles - 1

    def first_speeds(c):
        if c == 0:
            load(0)
        if c < last:
            load(c + 1)
        speeds(0, c)

    def next_speeds(step, c):
        sent_there(step - 1, c)
        speeds(step, c)

    for c in range(tiles):
        first_speeds(c)
        if c < 2:
            start_there(0, c)
    pier_means(0)
    for step in range(STEPS):
        for c in range(tiles):
            damp(step, c)
            if step == 0 and c + 2 < tiles:
                start_there(0, c + 2)
            if c == 0:
                pier_forces(step)
            if c == 2:
                pier_spread(step)
        more = step < STEPS - 1
        for c in range(tiles):
            arrive(step, c)
            if c > 0:
                edges(step, c - 1)
                shears(step, c - 1, more)
            if c > 1:
                normals(step, c - 2, more)
                if more:
                    next_speeds(step + 1, c - 2)
                    start_there(step + 1, c - 2)
        normals_last = last - 1
        if not more:
            normals(step, last - 1, more)
        edges(step, last)
        shears(step, last, more)
        if more:
            normals(step, last - 1, more)
            next_speeds(step + 1, last - 1)
            start_there(step + 1, last - 1)
        normals(step, last, more)
        if more:
            next_speeds(step + 1, last)
            start_there(step + 1, last)
            pier_means(step + 1)

    square[...] = jnp.zeros((LANES, LANES), f32)
    square[pl.ds(0, depth), :] = pltpu.roll(wbuf[...], lax.rem(LANES - g * own, LANES), 1)
    w_out[...] = jnp.transpose(square[...])[0:own, 0:depth]
    for c in range(tiles):
        sent_there(STEPS - 1, c)
        sent_back(STEPS - 1, c)


def deliver(v_ref, s_ref, w_ref, v_out, s_out, w_out, sem):
    depth, side = v_out.shape[1:3]
    inside = pl.ds(1, depth), pl.ds(ROWS, side)
    pairs = (
        (v_ref.at[(pl.ds(3 * (STEPS - 1), 3),) + inside], v_out),
        (s_ref.at[(pl.ds(0, 6),) + inside], s_out),
        (w_ref, w_out),
    )
    copies = [pltpu.make_async_copy(a, b, sem.at[i]) for i, (a, b) in enumerate(pairs)]
    for copy in copies:
        copy.start()
    for copy in copies:
        copy.wait()


def fused_body(
    n, ng, velocity, stress, pier_velocity, buoyancy, layer, lame_table, shear_table, relax_table,
    impedance, footprint, damp_inverse,
):
    depth, side, line = buoyancy.shape
    own = pier_velocity.shape[1]
    f32 = jnp.float32
    hbm = pl.BlockSpec(memory_space=pltpu.HBM)
    vmem = pl.BlockSpec(memory_space=pltpu.VMEM)
    smem = pl.BlockSpec(memory_space=pltpu.SMEM)
    dma = pltpu.SemaphoreType.DMA
    tall = side + 2 * ROWS
    stage = 2 * depth + ROWS
    tiles = line // LANES
    v, s, w = pl.pallas_call(
        functools.partial(fused, n, ng),
        out_shape=(
            pltpu.VMEM((3 * STEPS, depth + 2, tall, line), f32),
            pltpu.VMEM((6, depth + 2, tall, line), f32),
            pltpu.VMEM((own, depth), f32),
        ),
        in_specs=[hbm] * 3 + [smem] * 5 + [vmem, smem, vmem],
        out_specs=(vmem, vmem, vmem),
        scratch_shapes=[
            pltpu.VMEM((depth, side, line), f32),
            pltpu.VMEM((3, depth + 2, side, LANES), f32),
            pltpu.VMEM((3, depth, side, line), f32),
            pltpu.VMEM((3, n * depth, ROWS, LANES), f32),
            pltpu.VMEM((3, n * depth + 2, ROWS, LANES), f32),
            pltpu.VMEM((STEPS, ng, stage, LANES), f32),
            pltpu.VMEM((STEPS, n * depth, LANES), f32),
            pltpu.VMEM((depth, LANES), f32),
            pltpu.VMEM((LANES, LANES), f32),
            pltpu.VMEM((depth * side, LANES), f32),
            pltpu.VMEM((side, LANES), f32),
            pltpu.VMEM((tiles, 2 * LANES, LANES), jnp.bfloat16),
            pltpu.VMEM((2 * LANES, line), jnp.bfloat16),
            pltpu.VMEM(((depth + 2) * side, 2 * LANES), jnp.bfloat16),
            pltpu.VMEM((n * depth, 3 * n * depth), jnp.bfloat16),
            pltpu.VMEM((depth + ROWS, n * depth), f32),
            dma((3 * tiles,)), dma((3,)), dma((3,)), dma((2,)), dma((2,)), dma((3,)), dma((3,)),
            dma((STEPS, tiles)), dma((STEPS, tiles)), dma((STEPS, tiles)), dma((STEPS, tiles)),
            dma((STEPS,)), dma((STEPS,)), dma((STEPS,)), dma((STEPS,)),
            dma((STEPS, tiles, 2)), dma((STEPS, tiles, 2)),
        ],
        compiler_params=pltpu.CompilerParams(
            collective_id=0, has_side_effects=True, vmem_limit_bytes=48 * 1024 * 1024
        ),
    )(
        velocity, stress, buoyancy, layer, lame_table, shear_table, relax_table,
        footprint, pier_velocity.T, impedance, damp_inverse,
    )
    v, s, w = pl.pallas_call(
        deliver,
        out_shape=tuple(
            jax.ShapeDtypeStruct(a, f32) for a in (velocity.shape, stress.shape, (own, depth))
        ),
        in_specs=[vmem] * 3,
        out_specs=(hbm,) * 3,
        scratch_shapes=[dma((3,))],
        compiler_params=pltpu.CompilerParams(vmem_limit_bytes=8 * 1024 * 1024),
    )(v, s, w)
    return v, s, w.T


def whole_tiles(mesh, velocity, pier_velocity):
    n, ng = mesh.shape["gx"], mesh.shape["gy"]
    depth, side, line = velocity.shape[1] // n, velocity.shape[2] // ng, velocity.shape[3]
    return (
        line % LANES == 0
        and side % 16 == 0
        and side % n == 0
        and depth % ROWS == 0
        and (side // n) * (line // LANES) == ROWS
        and n * depth % LANES == 0
        and pier_velocity.shape[1] <= LANES
    )


def solution(mesh):
    placed = (
        P(None, "gx", "gy", None),
        P(None, "gx", "gy", None),
        P("gx", "gy"),
        P("gx", "gy", None),
        P("gx"),
        P(),
        P(),
        P(),
        P("gy"),
        P(),
        P(),
    )

    def run(*args):
        n, ng = mesh.shape["gx"], mesh.shape["gy"]
        if whole_tiles(mesh, args[0], args[2]):
            part = functools.partial(fused_body, n, ng)
        else:
            part = body
        return mapped(part)(*args)

    def mapped(part):
        return jax.shard_map(
            part,
            mesh=mesh,
            in_specs=placed,
            out_specs=(P(None, "gx", "gy", None), P(None, "gx", "gy", None), P("gx", "gy")),
            check_vma=False,
        )

    return run
```

time: 96.3 us -> 92.6 us (0.962)
  Pallas kernels: 95.5 us -> 91.7 us
    pallas_call x1, Pallas kernels: 93.2 us -> 89.4 us  [fused_body(): pl.pallas_call(functools.partial(fused, n, ng), out_shape=(pltpu.VMEM((3...]
where the time goes in v3:
time: 92.6 us; the launch traced here: 92.5 us
  Pallas kernels  91.7 us (99%)
    pallas_call x1, Pallas kernels, fused_body(): pl.pallas_call(functools.partial(fused, n, ng), out_shape=(pltpu.VMEM((3...  89.4 us
    pallas_call x1, Pallas kernels, fused_body(): pl.pallas_call(deliver, out_shape=tuple((jax.ShapeDtypeStruct(a, f32) for...  2.21 us

profile of v3, /device:TPU:0, one launch (start us, length us, event | category | flops | bytes accessed | tf_op | source)
XLA Modules:
  0.0 92.5 jit_solution(7973244653362561404)
XLA Ops:
  0.6 89.4 %shard_map.130 = (f32[6,18,32,512]{3,2,1,0:T(8,128)S(1)}, f32[6,18,32,512]{3,2,1,0:T(8,128)S(1)}, f32[4,16]{1,0:T(4,128)S(1)}) custom-call(f32[3,16,16,512]{3,2,1,0:T(8,128)} %v_hbm.1, f32[6,16,16,512]{3,2,1,0:T(8,128)} %s_hbm.1, f32[16,16,512]{2,1,0:T(8,128)} %b_hbm.1, s32[16]{0:T(128)} %layer_ref.1, f32[8]{0:T(128)} %lame_ref.1, f32[8]{0:T(128)} %shear_ref.1, ...), custom_call_target="tpu_custom_call" | custom-call | tf_op jit(solution)/shard_map/pallas_call | solution.py:706
  90.1 2.2 %shard_map.131 = (f32[3,16,16,512]{3,2,1,0:T(8,128)}, f32[6,16,16,512]{3,2,1,0:T(8,128)}, f32[4,16]{1,0:T(4,128)}) custom-call(f32[6,18,32,512]{3,2,1,0:T(8,128)S(1)} %get-tuple-element.9.v_ref, f32[6,18,32,512]{3,2,1,0:T(8,128)S(1)} %get-tuple-element.10.s_ref, f32[4,16]{1,0:T(4,128)S(1)} %get-tuple-element.11.w_ref), custom_call_target="tpu_custom_call" | custom-call | tf_op jit(solution)/shard_map/pallas_call | solution.py:744

commit v4 on v3

--- a/solution.py
+++ b/solution.py
@@ -181,9 +181,10 @@
 
 
 def fused(
-    n, ng, v_hbm, s_hbm, b_hbm, layer_ref, lame_ref, shear_ref, relax_ref, foot_ref, w_ref, imp_ref, damp_ref,
+    n, ng, v_hbm, s_hbm, b_hbm, layer_hbm, lame_hbm, shear_hbm, relax_hbm, foot_hbm, w_hbm, imp_hbm, damp_hbm,
     v_ext, s_ext, w_out,
-    buoy, coef, acc, pin, pout, um, fall, wbuf, square, part, rows_of, cols_t, cols_of, spread, damp_cat, damp_own,
+    layer_ref, lame_ref, shear_ref, relax_ref, foot_ref, w_ref, imp_ref, damp_ref, small_sem,
+    buoy, coef, acc, ahead_of, pin, pout, um, fall, wbuf, gain, square, part, rows_of, cols_t, cols_of, spread, damp_cat, damp_own,
     load_sem, zs_send, zs_recv, cf_send, cf_recv, ys_send, ys_recv,
     f_send, f_recv, r_send, r_recv, u_send, u_recv, p_send, p_recv, y_send, y_recv,
 ):
@@ -194,6 +195,7 @@
     share_rows = side // n
     inner = pl.ds(ROWS, side)
     own = w_ref.shape[0]
+    stage_rows = um.shape[2]
     f32, bf16 = jnp.float32, jnp.bfloat16
     above, below = ROWS - 1, ROWS + side
 
@@ -218,24 +220,15 @@
         for copy in loads[c]:
             copy.start()
 
-    plane = jnp.zeros((side, line), f32)
-    for f, way in Z_GHOSTS:
-        s_ext[f, 0 if way < 0 else depth + 1, inner, :] = plane
-    edge = jnp.zeros((depth + 2, line), f32)
-    for f, way in Y_GHOSTS:
-        s_ext[f, :, above if way < 0 else below, :] = edge
-    for f in range(3 * STEPS):
-        v_ext[f, :, above, :] = edge
-        v_ext[f, :, below, :] = edge
-    for k in range(depth):
-        for c, (table, scale) in enumerate(((lame_ref, grid_ratio), (shear_ref, grid_ratio), (relax_ref, 1.0))):
-            coef[c, k + 1] = jnp.full((side, LANES), scale * table[layer_ref[k]], f32)
-    for c in range(3):
-        coef[c, 0] = jnp.zeros((side, LANES), f32)
-        coef[c, depth + 1] = jnp.zeros((side, LANES), f32)
-        pout[c, 0] = jnp.zeros((ROWS, LANES), f32)
-        pout[c, n * depth + 1] = jnp.zeros((ROWS, LANES), f32)
-
+    smalls = [
+        pltpu.make_async_copy(src, dst, small_sem.at[i])
+        for i, (src, dst) in enumerate((
+            (layer_hbm, layer_ref), (lame_hbm, lame_ref), (shear_hbm, shear_ref), (relax_hbm, relax_ref),
+            (foot_hbm, foot_ref), (w_hbm, w_ref), (imp_hbm, imp_ref), (damp_hbm, damp_ref),
+        ))
+    ]
+    for copy in smalls:
+        copy.start()
     barrier = pltpu.get_barrier_semaphore()
     for d in range(1, n):
         pl.semaphore_signal(
@@ -280,52 +273,121 @@
     }
     ghosts = [(z_copy, i, not_ends[way][0:2]) for i, (f, way) in enumerate(Z_GHOSTS)]
     ghosts += [(y_stress, i, not_ends[way][2:4]) for i, (f, way) in enumerate(Y_GHOSTS)]
-    ghosts += [(c_copy, way, not_ends[way][0:2]) for way in (-1, 1)]
-    for make, i, (gets, sends) in ghosts:
-        @pl.when(sends)
-        def _(make=make, i=i):
-            make(i).start()
-
-    ids = lax.broadcasted_iota(jnp.int32, (side, LANES), 0) + g * side
-    lane_id = lax.broadcasted_iota(jnp.int32, (2 * LANES, LANES), 1)
-    row_id = lax.rem(lax.broadcasted_iota(jnp.int32, (2 * LANES, LANES), 0), LANES)
-    first = jnp.full((1, LANES), -64, jnp.int32)
-    begin_lane = jnp.full((1, LANES), -64, jnp.int32)
-    begin_row = jnp.full((2 * LANES, LANES), -64, jnp.int32)
-    for p in range(foot_ref.shape[0]):
-        first = jnp.where(lane_id[0:1] == p, foot_ref[p, 0] // line, first)
-        begin_lane = jnp.where(lane_id[0:1] == p, foot_ref[p, 0] % line, begin_lane)
-        begin_row = jnp.where(row_id == p, foot_ref[p, 0] % line, begin_row)
-    rows_of[...] = jnp.where((ids >= first) & (ids < first + SIDE), 1.0, 0.0)
-    for c in range(tiles):
-        at = row_id + c * LANES
-        cols_t[c] = jnp.where((at >= begin_lane) & (at < begin_lane + SIDE), 1.0, 0.0).astype(bf16)
-        at = lane_id + c * LANES
-        cols_of[:, lanes(c)] = jnp.where((at >= begin_row) & (at < begin_row + SIDE), 1.0, 0.0).astype(bf16)
+    layers = [(c_copy, way, not_ends[way][0:2]) for way in (-1, 1)]
+    def clear_stress():
+        edge = jnp.zeros((depth + 2, line), f32)
+
+        @pl.when(me == 0)
+        def _():
+            for f, way in Z_GHOSTS:
+                if way < 0:
+                    s_ext[f, 0, inner, :] = jnp.zeros((side, line), f32)
+
+        @pl.when(me == n - 1)
+        def _():
+            for f, way in Z_GHOSTS:
+                if way > 0:
+                    s_ext[f, depth + 1, inner, :] = jnp.zeros((side, line), f32)
+
+        @pl.when(g == 0)
+        def _():
+            for f, way in Y_GHOSTS:
+                if way < 0:
+                    s_ext[f, :, above, :] = edge
+
+        @pl.when(g == ng - 1)
+        def _():
+            for f, way in Y_GHOSTS:
+                if way > 0:
+                    s_ext[f, :, below, :] = edge
+
+    def clear_speeds():
+        edge = jnp.zeros((depth + 2, line), f32)
+
+        @pl.when(g == 0)
+        def _():
+            for f in range(3 * STEPS):
+                v_ext[f, :, above, :] = edge
+
+        @pl.when(g == ng - 1)
+        def _():
+            for f in range(3 * STEPS):
+                v_ext[f, :, below, :] = edge
+        for f in range(3):
+            pout[f, 0] = jnp.zeros((ROWS, LANES), f32)
+            pout[f, n * depth + 1] = jnp.zeros((ROWS, LANES), f32)
+
+    def set_layers():
+        for k in range(depth):
+            for c, (table, scale) in enumerate(((lame_ref, grid_ratio), (shear_ref, grid_ratio), (relax_ref, 1.0))):
+                coef[c, k + 1] = jnp.full((side, LANES), scale * table[layer_ref[k]], f32)
+        for end, k in ((0, 0), (n - 1, depth + 1)):
+            @pl.when(me == end)
+            def _(k=k):
+                for c in range(3):
+                    coef[c, k] = jnp.zeros((side, LANES), f32)
+        exchange(layers)
+
+    def exchange(copies):
+        for make, i, (gets, sends) in copies:
+            @pl.when(sends)
+            def _(make=make, i=i):
+                make(i).start()
+
+    def finish(copies):
+        for make, i, (gets, sends) in copies:
+            @pl.when(gets)
+            def _(make=make, i=i):
+                make(i).wait_recv()
+
+            @pl.when(sends)
+            def _(make=make, i=i):
+                make(i).wait_send()
+
+    def set_piers():
+        ids = lax.broadcasted_iota(jnp.int32, (side, LANES), 0) + g * side
+        lane_id = lax.broadcasted_iota(jnp.int32, (2 * LANES, LANES), 1)
+        row_id = lax.broadcasted_iota(jnp.int32, (2 * LANES, LANES), 0) & (LANES - 1)
+        first = jnp.full((1, LANES), -64, jnp.int32)
+        begin_lane = jnp.full((1, LANES), -64, jnp.int32)
+        begin_row = jnp.full((2 * LANES, LANES), -64, jnp.int32)
+        for p in range(foot_ref.shape[0]):
+            first = jnp.where(lane_id[0:1] == p, foot_ref[p, 0] // line, first)
+            begin_lane = jnp.where(lane_id[0:1] == p, foot_ref[p, 0] % line, begin_lane)
+            begin_row = jnp.where(row_id == p, foot_ref[p, 0] % line, begin_row)
+        rows_of[...] = jnp.where((ids >= first) & (ids < first + SIDE), 1.0, 0.0)
+        for c in range(tiles):
+            at = row_id + c * LANES
+            cols_t[c] = jnp.where((at >= begin_lane) & (at < begin_lane + SIDE), 1.0, 0.0).astype(bf16)
+            at = lane_id + c * LANES
+            cols_of[:, lanes(c)] = jnp.where((at >= begin_row) & (at < begin_row + SIDE), 1.0, 0.0).astype(bf16)
+        square[...] = jnp.zeros((LANES, LANES), f32)
+        square[pl.ds(0, own), pl.ds(0, depth)] = w_ref[...]
+        wbuf[...] = pltpu.roll(jnp.transpose(square[...])[0:depth], g * own, 1)
 
     def halves(a):
         high = a.astype(bf16)
         return high, (a - high.astype(f32)).astype(bf16)
 
-    high, low = halves(damp_ref[...])
-    damp_cat[...] = jnp.concatenate([high, high, low], axis=1)
-    damp_own[...] = jnp.zeros_like(damp_own)
-    damp_own[pl.ds(1, depth), :] = damp_ref[pl.ds(pl.multiple_of(me * depth, depth), depth), :]
-
-    @pl.when(me > 0)
-    def _():
-        damp_own[pl.ds(0, 1), :] = damp_ref[pl.ds(me * depth - 1, 1), :]
-
-    @pl.when(me < n - 1)
-    def _():
-        damp_own[pl.ds(depth + 1, 1), :] = damp_ref[pl.ds((me + 1) * depth, 1), :]
-
-    square[...] = jnp.zeros((LANES, LANES), f32)
-    square[pl.ds(0, own), pl.ds(0, depth)] = w_ref[...]
-    wbuf[...] = pltpu.roll(jnp.transpose(square[...])[0:depth], g * own, 1)
-    impedance = jnp.zeros((ROWS, LANES), f32)
-    for i in range(imp_ref.shape[0]):
-        impedance = jnp.where(lane_id[0:ROWS] == g * own + i, imp_ref[i], impedance)
+    def set_damping():
+        high, low = halves(damp_ref[...])
+        damp_cat[...] = jnp.concatenate([high, high, low], axis=1)
+        damp_own[...] = jnp.zeros_like(damp_own)
+        damp_own[pl.ds(1, depth), :] = damp_ref[pl.ds(pl.multiple_of(me * depth, depth), depth), :]
+
+        @pl.when(me > 0)
+        def _():
+            damp_own[pl.ds(0, 1), :] = damp_ref[pl.ds(me * depth - 1, 1), :]
+
+        @pl.when(me < n - 1)
+        def _():
+            damp_own[pl.ds(depth + 1, 1), :] = damp_ref[pl.ds((me + 1) * depth, 1), :]
+
+    def own_impedance():
+        impedance = jnp.zeros((ROWS, LANES), f32)
+        for i in range(imp_ref.shape[0]):
+            impedance = jnp.where(lax.broadcasted_iota(jnp.int32, (ROWS, LANES), 1) == g * own + i, imp_ref[i], impedance)
+        return impedance
 
     def look(ref, f, k, count, c, dy=0, dz=0):
         return ref[f, pl.ds(k + dz, count), pl.ds(ROWS + dy, side), lanes(c)].reshape(count * side, LANES)
@@ -357,6 +419,57 @@
 
     def put(ref, f, k, count, c, value):
         ref[f, pl.ds(k, count), inner, lanes(c)] = value.reshape(count, side, LANES)
+
+    def early_speeds():
+        def run(i, carry):
+            k, count = 2 + 2 * i, 2
+            at = functools.partial(look, s_ext)
+            size = count * side
+            scaled = grid_ratio * buoy[pl.ds(k - 1, count), :, lanes(0)].reshape(size, LANES)
+            xx, yy, zz, xy, xz, yz = (at(f, k, count, 0) for f in range(6))
+            total = (xx - behind(lambda c: at(0, k, count, c), 0)) + (pltpu.roll(xy, size - 1, 0) - xy)
+            total = total + (at(4, k, count, 0, 0, 1) - xz)
+            values = [total]
+            total = (ahead(lambda c: at(3, k, count, c), 0) - xy) + (yy - pltpu.roll(yy, 1, 0))
+            values.append(total + (at(5, k, count, 0, 0, 1) - yz))
+            total = (ahead(lambda c: at(4, k, count, c), 0) - xz) + (pltpu.roll(yz, size - 1, 0) - yz)
+            values.append(total + (zz - at(2, k, count, 0, 0, -1)))
+            for f in range(3):
+                value = look(v_ext, f, k, count, 0) + scaled * values[f]
+                ahead_of[f, pl.ds(k - 1, count)] = value.reshape(count, side, LANES)
+            return carry
+
+        lax.fori_loop(0, (depth - 2) // 2, run, 0)
+
+    def inner_peer(d):
+        t = lax.rem(me + d, n)
+        return t, (t > 0) & (t < n - 1)
+
+    def early_copy(d, ref, low, count, at):
+        t = lax.rem(me + d, n)
+        return pltpu.make_async_remote_copy(
+            src_ref=ref.at[:, pl.ds(low, count), mine(t), at],
+            dst_ref=pin.at[:, pl.ds(me * depth + low, count), mine(0), :],
+            send_sem=f_send.at[0, 0], recv_sem=f_recv.at[0, 0], device_id=(t, g), device_id_type=MESH,
+        )
+
+    def early_there():
+        for d in range(1, n):
+            @pl.when(inner_peer(d)[1])
+            def _(d=d):
+                early_copy(d, ahead_of, 1, depth - 2, pl.ds(0, LANES)).start()
+
+    def late_there():
+        for d in range(1, n):
+            @pl.when(inner_peer(d)[1])
+            def _(d=d):
+                early_copy(d, acc, 0, 1, lanes(0)).start()
+                early_copy(d, acc, depth - 1, 1, lanes(0)).start()
+
+            @pl.when(jnp.logical_not(inner_peer(d)[1]))
+            def _(d=d):
+                there(0, 0, d).start()
+        there(0, 0, 0).start()
 
     def speeds(step, c):
         base = 3 * (step - 1) if step > 0 else 0
@@ -377,6 +490,8 @@
                 acc[f, pl.ds(k - 1, count), :, lanes(c)] = value.reshape(count, side, LANES)
 
         blocks(run)
+
+    def pier_part(c):
         high, low = halves(acc[2, :, :, lanes(c)].reshape(depth * side, LANES))
         term = jnp.dot(jnp.concatenate([high, low], axis=1), cols_t[c], preferred_element_type=f32)
         part[...] = term if c == 0 else part[...] + term
@@ -516,9 +631,12 @@
                 pout[f, pl.ds(1, n * depth), share_rows * c + r, :] = damped[:, r * LANES : (r + 1) * LANES]
         start_back(step, c)
 
+    def shared(step):
+        return pl.ds(0, stage_rows if step == 0 else depth)
+
     def share(step, d):
         return pltpu.make_async_remote_copy(
-            src_ref=um.at[step, 0], dst_ref=um.at[step, d],
+            src_ref=um.at[step, 0, shared(step)], dst_ref=um.at[step, d, shared(step)],
             send_sem=u_send.at[step], recv_sem=u_recv.at[step],
             device_id=(me, lax.rem(g + d, ng)), device_id_type=MESH,
         )
@@ -534,19 +652,23 @@
     def pier_means(step):
         masked = part[...].reshape(depth, side, LANES) * rows_of[...][None]
         um[step, 0, pl.ds(0, depth), :] = jnp.sum(masked, axis=1)
-        um[step, 0, pl.ds(depth, depth), :] = wbuf[...]
-        um[step, 0, pl.ds(2 * depth, ROWS), :] = impedance
+        if step == 0:
+            um[step, 0, pl.ds(depth, depth), :] = wbuf[...]
+            um[step, 0, pl.ds(2 * depth, ROWS), :] = own_impedance()
         for d in range(1, ng):
             share(step, d).start()
 
     def pier_forces(step):
-        settle(um.at[step, pl.ds(1, ng - 1)], u_recv.at[step])
-        settle(um.at[step, pl.ds(1, ng - 1)], u_send.at[step])
-        every = um[step, 0]
+        settle(um.at[step, pl.ds(1, ng - 1), shared(step)], u_recv.at[step])
+        settle(um.at[step, pl.ds(1, ng - 1), shared(step)], u_send.at[step])
+        every = um[step, 0, shared(step), :]
         for d in range(1, ng):
-            every = every + um[step, d]
-        w = every[depth : 2 * depth] if step == 0 else wbuf[...]
-        force = every[2 * depth : 2 * depth + 1] * (w - every[0:depth] / FOOT)
+            every = every + um[step, d, shared(step), :]
+        if step == 0:
+            wbuf[...] = every[depth : 2 * depth]
+            gain[...] = every[2 * depth :]
+        w = wbuf[...]
+        force = gain[0:1, :] * (w - every[0:depth] / FOOT)
         wbuf[...] = w - pier_gain * force
         fall[step, pl.ds(pl.multiple_of(me * depth, depth), depth), :] = soil_gain * force
         for d in range(1, n):
@@ -604,67 +726,92 @@
         for copy in loads[c]:
             copy.wait()
 
-    for make, i, (gets, sends) in ghosts:
-        @pl.when(gets)
-        def _(make=make, i=i):
-            make(i).wait_recv()
-
-        @pl.when(sends)
-        def _(make=make, i=i):
-            make(i).wait_send()
-
     last = tiles - 1
 
     def first_speeds(c):
-        if c == 0:
-            load(0)
-        if c < last:
+        if 0 < c < last:
             load(c + 1)
         speeds(0, c)
 
     def next_speeds(step, c):
         sent_there(step - 1, c)
         speeds(step, c)
-
+        if c == last:
+            pier_part(c)
+            pier_means(step)
+        start_there(step, c)
+        if c < last:
+            pier_part(c)
+
+    exchange(ghosts)
+    for copy in smalls:
+        copy.wait()
+    load(0)
+    load(1)
+    early_speeds()
+    early_there()
+    clear_stress()
+    finish(ghosts)
+    first_speeds(0)
+    late_there()
+    set_piers()
+    for c in range(1, tiles):
+        first_speeds(c)
     for c in range(tiles):
-        first_speeds(c)
-        if c < 2:
-            start_there(0, c)
+        pier_part(c)
     pier_means(0)
-    for step in range(STEPS):
-        for c in range(tiles):
-            damp(step, c)
-            if step == 0 and c + 2 < tiles:
-                start_there(0, c + 2)
-            if c == 0:
-                pier_forces(step)
-            if c == 2:
-                pier_spread(step)
-        more = step < STEPS - 1
-        for c in range(tiles):
-            arrive(step, c)
-            if c > 0:
-                edges(step, c - 1)
-                shears(step, c - 1, more)
-            if c > 1:
-                normals(step, c - 2, more)
-                if more:
-                    next_speeds(step + 1, c - 2)
-                    start_there(step + 1, c - 2)
-        normals_last = last - 1
-        if not more:
-            normals(step, last - 1, more)
-        edges(step, last)
-        shears(step, last, more)
-        if more:
-            normals(step, last - 1, more)
-            next_speeds(step + 1, last - 1)
-            start_there(step + 1, last - 1)
-        normals(step, last, more)
-        if more:
-            next_speeds(step + 1, last)
-            start_there(step + 1, last)
-            pier_means(step + 1)
+    start_there(0, 1)
+    set_layers()
+    set_damping()
+    clear_speeds()
+
+    def next_stress(c):
+        normals(0, c, True)
+        next_speeds(1, c)
+
+    def bend(step, c):
+        edges(step, c)
+        shears(step, c, step < STEPS - 1)
+
+    pier_forces(0)
+    damp(0, 0)
+    start_there(0, 2)
+    damp(0, 1)
+    start_there(0, 3)
+    pier_spread(0)
+    damp(0, 2)
+    damp(0, 3)
+    finish(layers)
+    arrive(0, 0)
+    arrive(0, 1)
+    bend(0, 0)
+    arrive(0, 2)
+    bend(0, 1)
+    next_stress(0)
+    arrive(0, 3)
+    bend(0, 2)
+    next_stress(1)
+    bend(0, 3)
+    next_stress(2)
+    next_stress(3)
+    damp(1, 0)
+    pier_forces(1)
+    damp(1, 1)
+    damp(1, 2)
+    pier_spread(1)
+    damp(1, 3)
+    arrive(1, 0)
+    arrive(1, 1)
+    bend(1, 0)
+    arrive(1, 2)
+    bend(1, 1)
+    normals(1, 0, False)
+    arrive(1, 3)
+    bend(1, 2)
+    normals(1, 1, False)
+    normals(1, 2, False)
+    bend(1, 3)
+    normals(1, 3, False)
 
     square[...] = jnp.zeros((LANES, LANES), f32)
     square[pl.ds(0, depth), :] = pltpu.roll(wbuf[...], lax.rem(LANES - g * own, LANES), 1)
@@ -677,11 +824,9 @@
 def deliver(v_ref, s_ref, w_ref, v_out, s_out, w_out, sem):
     depth, side = v_out.shape[1:3]
     inside = pl.ds(1, depth), pl.ds(ROWS, side)
-    pairs = (
-        (v_ref.at[(pl.ds(3 * (STEPS - 1), 3),) + inside], v_out),
-        (s_ref.at[(pl.ds(0, 6),) + inside], s_out),
-        (w_ref, w_out),
-    )
+    pairs = [(w_ref, w_out)]
+    pairs += [(s_ref.at[(f,) + inside], s_out.at[f]) for f in range(6)]
+    pairs += [(v_ref.at[(3 * (STEPS - 1) + f,) + inside], v_out.at[f]) for f in range(3)]
     copies = [pltpu.make_async_copy(a, b, sem.at[i]) for i, (a, b) in enumerate(pairs)]
     for copy in copies:
         copy.start()
@@ -698,7 +843,6 @@
     f32 = jnp.float32
     hbm = pl.BlockSpec(memory_space=pltpu.HBM)
     vmem = pl.BlockSpec(memory_space=pltpu.VMEM)
-    smem = pl.BlockSpec(memory_space=pltpu.SMEM)
     dma = pltpu.SemaphoreType.DMA
     tall = side + 2 * ROWS
     stage = 2 * depth + ROWS
@@ -710,17 +854,28 @@
             pltpu.VMEM((6, depth + 2, tall, line), f32),
             pltpu.VMEM((own, depth), f32),
         ),
-        in_specs=[hbm] * 3 + [smem] * 5 + [vmem, smem, vmem],
+        in_specs=[hbm] * 11,
         out_specs=(vmem, vmem, vmem),
         scratch_shapes=[
+            pltpu.SMEM(layer.shape, layer.dtype),
+            pltpu.SMEM(lame_table.shape, f32),
+            pltpu.SMEM(shear_table.shape, f32),
+            pltpu.SMEM(relax_table.shape, f32),
+            pltpu.SMEM(footprint.shape, footprint.dtype),
+            pltpu.VMEM((own, depth), f32),
+            pltpu.SMEM(impedance.shape, f32),
+            pltpu.VMEM(damp_inverse.shape, f32),
+            dma((8,)),
             pltpu.VMEM((depth, side, line), f32),
             pltpu.VMEM((3, depth + 2, side, LANES), f32),
             pltpu.VMEM((3, depth, side, line), f32),
+            pltpu.VMEM((3, depth, side, LANES), f32),
             pltpu.VMEM((3, n * depth, ROWS, LANES), f32),
             pltpu.VMEM((3, n * depth + 2, ROWS, LANES), f32),
             pltpu.VMEM((STEPS, ng, stage, LANES), f32),
             pltpu.VMEM((STEPS, n * depth, LANES), f32),
             pltpu.VMEM((depth, LANES), f32),
+            pltpu.VMEM((ROWS, LANES), f32),
             pltpu.VMEM((LANES, LANES), f32),
             pltpu.VMEM((depth * side, LANES), f32),
             pltpu.VMEM((side, LANES), f32),
@@ -748,7 +903,7 @@
         ),
         in_specs=[vmem] * 3,
         out_specs=(hbm,) * 3,
-        scratch_shapes=[dma((3,))],
+        scratch_shapes=[dma((10,))],
         compiler_params=pltpu.CompilerParams(vmem_limit_bytes=8 * 1024 * 1024),
     )(v, s, w)
     return v, s, w.T

time: 92.6 us -> 90.4 us (0.976)
  Pallas kernels: 91.7 us -> 89.5 us
    pallas_call x1, Pallas kernels: 89.4 us -> 87.2 us  [fused_body(): pl.pallas_call(functools.partial(fused, n, ng), out_shape=(pltpu.VMEM((3...]
where the time goes in v4:
time: 90.4 us; the launch traced here: 90.3 us
  Pallas kernels  89.5 us (99%)
    pallas_call x1, Pallas kernels, fused_body(): pl.pallas_call(functools.partial(fused, n, ng), out_shape=(pltpu.VMEM((3...  87.2 us
    pallas_call x1, Pallas kernels, fused_body(): pl.pallas_call(deliver, out_shape=tuple((jax.ShapeDtypeStruct(a, f32) for...  2.26 us

profile of v4, /device:TPU:0, one launch (start us, length us, event | category | flops | bytes accessed | tf_op | source)
XLA Modules:
  0.0 90.3 jit_solution(678204400925940908)
XLA Ops:
  0.6 87.2 %shard_map.130 = (f32[6,18,32,512]{3,2,1,0:T(8,128)S(1)}, f32[6,18,32,512]{3,2,1,0:T(8,128)S(1)}, f32[4,16]{1,0:T(4,128)S(1)}) custom-call(f32[3,16,16,512]{3,2,1,0:T(8,128)} %v_hbm.1, f32[6,16,16,512]{3,2,1,0:T(8,128)} %s_hbm.1, f32[16,16,512]{2,1,0:T(8,128)} %b_hbm.1, s32[16]{0:T(128)} %layer_hbm.1, f32[8]{0:T(128)} %lame_hbm.1, f32[8]{0:T(128)} %shear_hbm.1, ...), custom_call_target="tpu_custom_call" | custom-call | tf_op jit(solution)/shard_map/pallas_call | solution.py:850
  87.9 2.3 %shard_map.131 = (f32[3,16,16,512]{3,2,1,0:T(8,128)}, f32[6,16,16,512]{3,2,1,0:T(8,128)}, f32[4,16]{1,0:T(4,128)}) custom-call(f32[6,18,32,512]{3,2,1,0:T(8,128)S(1)} %get-tuple-element.9.v_ref, f32[6,18,32,512]{3,2,1,0:T(8,128)S(1)} %get-tuple-element.10.s_ref, f32[4,16]{1,0:T(4,128)S(1)} %get-tuple-element.11.w_ref), custom_call_target="tpu_custom_call" | custom-call | tf_op jit(solution)/shard_map/pallas_call | solution.py:899

commit v5 on v4

--- a/solution.py
+++ b/solution.py
@@ -450,7 +450,7 @@
         return pltpu.make_async_remote_copy(
             src_ref=ref.at[:, pl.ds(low, count), mine(t), at],
             dst_ref=pin.at[:, pl.ds(me * depth + low, count), mine(0), :],
-            send_sem=f_send.at[0, 0], recv_sem=f_recv.at[0, 0], device_id=(t, g), device_id_type=MESH,
+            send_sem=f_send.at[0], recv_sem=f_recv.at[0], device_id=(t, g), device_id_type=MESH,
         )
 
     def early_there():
@@ -565,10 +565,10 @@
         src = acc.at[:, :, mine(t), lanes(c)]
         dst = pin.at[:, pl.ds(me * depth, depth), mine(c), :]
         if d == 0:
-            return pltpu.make_async_copy(src, dst, f_recv.at[step, c])
+            return pltpu.make_async_copy(src, dst, f_recv.at[c])
         return pltpu.make_async_remote_copy(
-            src_ref=src, dst_ref=dst, send_sem=f_send.at[step, c],
-            recv_sem=f_recv.at[step, c], device_id=(t, g), device_id_type=MESH,
+            src_ref=src, dst_ref=dst, send_sem=f_send.at[c],
+            recv_sem=f_recv.at[c], device_id=(t, g), device_id_type=MESH,
         )
 
     def back(step, c, d):
@@ -583,11 +583,11 @@
                 pl.ds(3 * step + f, fields), pl.ds(low, count), pl.ds(ROWS + me * share_rows, share_rows), lanes(c)
             ]
             if d == 0:
-                copies.append(pltpu.make_async_copy(src, dst, r_recv.at[step, c]))
+                copies.append(pltpu.make_async_copy(src, dst, r_recv.at[c]))
             else:
                 copies.append(pltpu.make_async_remote_copy(
-                    src_ref=src, dst_ref=dst, send_sem=r_send.at[step, c],
-                    recv_sem=r_recv.at[step, c], device_id=(t, g), device_id_type=MESH,
+                    src_ref=src, dst_ref=dst, send_sem=r_send.at[c],
+                    recv_sem=r_recv.at[c], device_id=(t, g), device_id_type=MESH,
                 ))
         return copies
 
@@ -604,17 +604,17 @@
                 copy.start()
 
     def sent_there(step, c):
-        settle(pin.at[:, pl.ds(0, (n - 1) * depth), mine(c), :], f_send.at[step, c])
+        settle(pin.at[:, pl.ds(0, (n - 1) * depth), mine(c), :], f_send.at[c])
 
     def got_there(step, c):
-        settle(pin.at[:, :, mine(c), :], f_recv.at[step, c])
+        settle(pin.at[:, :, mine(c), :], f_recv.at[c])
 
     def sent_back(step, c):
-        settle(pout.at[:, pl.ds(0, (n - 1) * count_back(step)), mine(c), :], r_send.at[step, c])
+        settle(pout.at[:, pl.ds(0, (n - 1) * count_back(step)), mine(c), :], r_send.at[c])
 
     def got_back(step, c):
         settle(
-            v_ext.at[pl.ds(3 * step, 3), pl.ds(0, count_back(step)), inner, lanes(c)], r_recv.at[step, c]
+            v_ext.at[pl.ds(3 * step, 3), pl.ds(0, count_back(step)), inner, lanes(c)], r_recv.at[c]
         )
 
     def damp(step, c):
@@ -686,10 +686,12 @@
     def y_speed(step, c, i):
         low, count = (0, depth + 2) if step < STEPS - 1 else (1, depth)
         fields, planes = pl.ds(3 * step, 3), pl.ds(low, count)
+        if step == STEPS - 1 and i == 1:
+            fields = pl.ds(3 * step + 1, 1)
         return pltpu.make_async_remote_copy(
             src_ref=v_ext.at[fields, planes, pl.ds(below - 1 if i == 0 else ROWS, 1), lanes(c)],
             dst_ref=v_ext.at[fields, planes, pl.ds(above if i == 0 else below, 1), lanes(c)],
-            send_sem=y_send.at[step, c, i], recv_sem=y_recv.at[step, c, i],
+            send_sem=y_send.at[c, i], recv_sem=y_recv.at[c, i],
             device_id=(me, g + 1 - 2 * i), device_id_type=MESH,
         )
 
@@ -754,13 +756,14 @@
     finish(ghosts)
     first_speeds(0)
     late_there()
+    first_speeds(1)
+    start_there(0, 1)
     set_piers()
-    for c in range(1, tiles):
+    for c in range(2, tiles):
         first_speeds(c)
     for c in range(tiles):
         pier_part(c)
     pier_means(0)
-    start_there(0, 1)
     set_layers()
     set_damping()
     clear_speeds()
@@ -824,9 +827,11 @@
 def deliver(v_ref, s_ref, w_ref, v_out, s_out, w_out, sem):
     depth, side = v_out.shape[1:3]
     inside = pl.ds(1, depth), pl.ds(ROWS, side)
-    pairs = [(w_ref, w_out)]
-    pairs += [(s_ref.at[(f,) + inside], s_out.at[f]) for f in range(6)]
-    pairs += [(v_ref.at[(3 * (STEPS - 1) + f,) + inside], v_out.at[f]) for f in range(3)]
+    pairs = (
+        (s_ref.at[(pl.ds(0, 6),) + inside], s_out),
+        (v_ref.at[(pl.ds(3 * (STEPS - 1), 3),) + inside], v_out),
+        (w_ref, w_out),
+    )
     copies = [pltpu.make_async_copy(a, b, sem.at[i]) for i, (a, b) in enumerate(pairs)]
     for copy in copies:
         copy.start()
@@ -885,9 +890,9 @@
             pltpu.VMEM((n * depth, 3 * n * depth), jnp.bfloat16),
             pltpu.VMEM((depth + ROWS, n * depth), f32),
             dma((3 * tiles,)), dma((3,)), dma((3,)), dma((2,)), dma((2,)), dma((3,)), dma((3,)),
-            dma((STEPS, tiles)), dma((STEPS, tiles)), dma((STEPS, tiles)), dma((STEPS, tiles)),
+            dma((tiles,)), dma((tiles,)), dma((tiles,)), dma((tiles,)),
             dma((STEPS,)), dma((STEPS,)), dma((STEPS,)), dma((STEPS,)),
-            dma((STEPS, tiles, 2)), dma((STEPS, tiles, 2)),
+            dma((tiles, 2)), dma((tiles, 2)),
         ],
         compiler_params=pltpu.CompilerParams(
             collective_id=0, has_side_effects=True, vmem_limit_bytes=48 * 1024 * 1024
@@ -903,7 +908,7 @@
         ),
         in_specs=[vmem] * 3,
         out_specs=(hbm,) * 3,
-        scratch_shapes=[dma((10,))],
+        scratch_shapes=[dma((3,))],
         compiler_params=pltpu.CompilerParams(vmem_limit_bytes=8 * 1024 * 1024),
     )(v, s, w)
     return v, s, w.T

time: 90.4 us -> 88.9 us (0.983)
  Pallas kernels: 89.5 us -> 87.9 us
    pallas_call x1, Pallas kernels: 87.2 us -> 85.7 us  [fused_body(): pl.pallas_call(functools.partial(fused, n, ng), out_shape=(pltpu.VMEM((3...]
where the time goes in v5:
time: 88.9 us; the launch traced here: 88.7 us
  Pallas kernels  87.9 us (99%)
    pallas_call x1, Pallas kernels, fused_body(): pl.pallas_call(functools.partial(fused, n, ng), out_shape=(pltpu.VMEM((3...  85.7 us
    pallas_call x1, Pallas kernels, fused_body(): pl.pallas_call(deliver, out_shape=tuple((jax.ShapeDtypeStruct(a, f32) for...  2.21 us

profile of v5, /device:TPU:0, one launch (start us, length us, event | category | flops | bytes accessed | tf_op | source)
XLA Modules:
  0.0 88.7 jit_solution(2902241643663313943)
XLA Ops:
  0.6 85.7 %shard_map.130 = (f32[6,18,32,512]{3,2,1,0:T(8,128)S(1)}, f32[6,18,32,512]{3,2,1,0:T(8,128)S(1)}, f32[4,16]{1,0:T(4,128)S(1)}) custom-call(f32[3,16,16,512]{3,2,1,0:T(8,128)} %v_hbm.1, f32[6,16,16,512]{3,2,1,0:T(8,128)} %s_hbm.1, f32[16,16,512]{2,1,0:T(8,128)} %b_hbm.1, s32[16]{0:T(128)} %layer_hbm.1, f32[8]{0:T(128)} %lame_hbm.1, f32[8]{0:T(128)} %shear_hbm.1, ...), custom_call_target="tpu_custom_call" | custom-call | tf_op jit(solution)/shard_map/pallas_call | solution.py:855
  86.3 2.2 %shard_map.131 = (f32[3,16,16,512]{3,2,1,0:T(8,128)}, f32[6,16,16,512]{3,2,1,0:T(8,128)}, f32[4,16]{1,0:T(4,128)}) custom-call(f32[6,18,32,512]{3,2,1,0:T(8,128)S(1)} %get-tuple-element.9.v_ref, f32[6,18,32,512]{3,2,1,0:T(8,128)S(1)} %get-tuple-element.10.s_ref, f32[4,16]{1,0:T(4,128)S(1)} %get-tuple-element.11.w_ref), custom_call_target="tpu_custom_call" | custom-call | tf_op jit(solution)/shard_map/pallas_call | solution.py:904

commit v6 on v5

--- a/solution.py
+++ b/solution.py
@@ -803,6 +803,11 @@
     damp(1, 2)
     pier_spread(1)
     damp(1, 3)
+    square[...] = jnp.zeros((LANES, LANES), f32)
+    square[pl.ds(0, depth), :] = pltpu.roll(wbuf[...], lax.rem(LANES - g * own, LANES), 1)
+    w_out[...] = jnp.transpose(square[...])[0:own, 0:depth]
+    for c in range(tiles):
+        sent_there(STEPS - 1, c)
     arrive(1, 0)
     arrive(1, 1)
     bend(1, 0)
@@ -816,11 +821,7 @@
     bend(1, 3)
     normals(1, 3, False)
 
-    square[...] = jnp.zeros((LANES, LANES), f32)
-    square[pl.ds(0, depth), :] = pltpu.roll(wbuf[...], lax.rem(LANES - g * own, LANES), 1)
-    w_out[...] = jnp.transpose(square[...])[0:own, 0:depth]
     for c in range(tiles):
-        sent_there(STEPS - 1, c)
         sent_back(STEPS - 1, c)
 
 

time: 88.9 us -> 88.7 us (level)
  no operation moved by 1% of the time
where the time goes in v6:
time: 88.7 us; the launch traced here: 88.6 us
  Pallas kernels  87.8 us (99%)
    pallas_call x1, Pallas kernels, fused_body(): pl.pallas_call(functools.partial(fused, n, ng), out_shape=(pltpu.VMEM((3...  85.6 us
    pallas_call x1, Pallas kernels, fused_body(): pl.pallas_call(deliver, out_shape=tuple((jax.ShapeDtypeStruct(a, f32) for...  2.21 us

profile of v6, /device:TPU:0, one launch (start us, length us, event | category | flops | bytes accessed | tf_op | source)
XLA Modules:
  0.0 88.6 jit_solution(6721175864605473520)
XLA Ops:
  0.6 85.6 %shard_map.130 = (f32[6,18,32,512]{3,2,1,0:T(8,128)S(1)}, f32[6,18,32,512]{3,2,1,0:T(8,128)S(1)}, f32[4,16]{1,0:T(4,128)S(1)}) custom-call(f32[3,16,16,512]{3,2,1,0:T(8,128)} %v_hbm.1, f32[6,16,16,512]{3,2,1,0:T(8,128)} %s_hbm.1, f32[16,16,512]{2,1,0:T(8,128)} %b_hbm.1, s32[16]{0:T(128)} %layer_hbm.1, f32[8]{0:T(128)} %lame_hbm.1, f32[8]{0:T(128)} %shear_hbm.1, ...), custom_call_target="tpu_custom_call" | custom-call | tf_op jit(solution)/shard_map/pallas_call | solution.py:856
  86.2 2.2 %shard_map.131 = (f32[3,16,16,512]{3,2,1,0:T(8,128)}, f32[6,16,16,512]{3,2,1,0:T(8,128)}, f32[4,16]{1,0:T(4,128)}) custom-call(f32[6,18,32,512]{3,2,1,0:T(8,128)S(1)} %get-tuple-element.9.v_ref, f32[6,18,32,512]{3,2,1,0:T(8,128)S(1)} %get-tuple-element.10.s_ref, f32[4,16]{1,0:T(4,128)S(1)} %get-tuple-element.11.w_ref), custom_call_target="tpu_custom_call" | custom-call | tf_op jit(solution)/shard_map/pallas_call | solution.py:905
